TPU v7x, 128 devices: a whole 4x4x4 slice. The times are simulated.
128 devices in a mesh: seq: 16 (over z, y), chan: 8 (over x, core).
Axes of the slice: x: 4, y: 4, z: 4, core: 2. Of those that a mesh axis runs over, the one named last changes fastest.
Arguments:
- inputs: bfloat16 [8192, 4096], P('seq', 'chan'), may hold values from -6 to 6
- out_grad: bfloat16 [8192, 4096], P('seq', 'chan'), may hold values from -0.0034179688 to 0.0034179688
- embed_weight: float32 [17, 64], replicated, may hold values from -1.5 to 1.5
- embed_bias: float32 [64], replicated, may hold values from -1 to 1
- embed_freq: float32 [64], replicated, may hold values from 0.5 to 2
- mixer_weight: float32 [64, 64], replicated, may hold values from -0.75 to 0.75
- mixer_bias: float32 [64], replicated, may hold values from -1 to 1
- mixer_freq: float32 [64], replicated, may hold values from 0.5 to 2
- head_weight: float32 [64, 4096], P(None, 'chan'), may hold values from -0.75 to 0.75
- decay_rates: float32 [4096], P('chan'), may hold values from 1 to 12
Outputs:
- embed_weight_grad: float32 [17, 64], replicated
- embed_bias_grad: float32 [64], replicated
- embed_freq_grad: float32 [64], replicated
- mixer_weight_grad: float32 [64, 64], replicated
- mixer_bias_grad: float32 [64], replicated
- mixer_freq_grad: float32 [64], replicated
- head_weight_grad: float32 [64, 4096], P(None, 'chan')
- decay_rates_grad: float32 [4096], P('chan')
All inputs are finite; a program needn't handle non-finite values.
Results may differ from a plain program's by a relative error of at most 0.0003.
Values may be sent and summed in bfloat16 or wider, within the bound.
A program may use at most 128 MiB of HBM per device.

v0:
```python
import math

import jax
import jax.numpy as jnp
import numpy as np
from jax import lax
from jax.experimental import pallas as pl
from jax.experimental.pallas import tpu as pltpu
from jax.sharding import PartitionSpec as P

MESH = pl.DeviceIdType.MESH
EXACT = lax.Precision.HIGHEST
F32 = jnp.float32
BF16 = jnp.bfloat16

FILTER_LEN = 1536
BANDS = 8
FEATURES = 17
FEATURE_ROWS = 24
HIDDEN = 64
BLOCK = 512
SEQ = 16
CHAN = 8
OWN = 32
PARTS = 3
SEQ_SIDE = 4


def transform_table():
    order = np.concatenate([np.arange(0, BLOCK, 2), np.arange(1, BLOCK, 2)])
    turns = (2 * order[None, :] + 1) * np.arange(BLOCK)[:, None] % (4 * BLOCK)
    angle = turns * (2.0 * math.pi / (4 * BLOCK))
    table = np.concatenate([np.cos(angle), -np.sin(angle)], axis=1)
    high = table.astype(BF16)
    low = (table - high.astype(np.float64)).astype(BF16)
    return high, low


def tap_table():
    taps = np.arange(FILTER_LEN)
    freqs = np.array([max(1, FILTER_LEN // 4 // 2 ** (BANDS - level)) for level in range(1, BANDS + 1)])
    angle = (freqs[:, None] * taps[None, :] % FILTER_LEN) * (2.0 * math.pi / FILTER_LEN)
    table = np.zeros((FEATURE_ROWS, FILTER_LEN), np.float32)
    table[0] = taps / FILTER_LEN
    table[1 : 1 + BANDS] = np.cos(angle)
    table[1 + BANDS : FEATURES] = np.sin(angle)
    table[FEATURES] = 1.0
    return table


def dot(a, b, a_dim=1, b_dim=0, precision=EXACT):
    return lax.dot_general(
        a, b, (((a_dim,), (b_dim,)), ((), ())), precision=precision, preferred_element_type=F32
    )


def sin_cos(a):
    turns = jnp.floor(a * (2.0 / math.pi) + 0.5)
    r = a - turns * 1.5703125
    r = r - turns * 4.837512969970703125e-4
    r = r - turns * 7.549789954891882e-8
    r2 = r * r
    s = r + r * r2 * (-1.6666654611e-1 + r2 * (8.3321608736e-3 + r2 * -1.9515295891e-4))
    c = 1.0 - 0.5 * r2 + r2 * r2 * (4.166664568298827e-2 + r2 * (-1.388731625493765e-3 + r2 * 2.443315711809948e-5))
    q = turns.astype(jnp.int32)
    odd = (q & 1) == 1
    sine = jnp.where(odd, c, s)
    cosine = jnp.where(odd, s, c)
    sine = jnp.where((q & 2) == 2, -sine, sine)
    cosine = jnp.where(((q + 1) & 2) == 2, -cosine, cosine)
    return sine, cosine


def column(row):
    n = row.shape[1]
    hit = lax.broadcasted_iota(jnp.int32, (n, n), 0) == lax.broadcasted_iota(jnp.int32, (n, n), 1)
    return jnp.sum(jnp.where(hit, row, 0.0), axis=1, keepdims=True)


def kernel(
    x_hbm, g_hbm, ew, eb, ef, mw, mb, mf, hw, dr, high_hbm, low_hbm, feat,
    ew_out, eb_out, ef_out, mw_out, mb_out, mf_out, hw_out, dr_out,
    x_in, g_in, high, low, send, recv, spec, prod, lags,
    first_pre, first_cos, first_act, second_pre, second_cos, second_act, shaped, envelope,
    head_all, part, sum_recv, tile, tile_recv, total,
    local_sem, a2a_send, a2a_recv, head_send, head_recv, sum_send, sum_got, tile_send, tile_got, all_send, all_got,
):
    s = lax.axis_index("seq")
    c = lax.axis_index("chan")
    z = s // SEQ_SIDE
    y = s % SEQ_SIDE

    loads = [
        pltpu.make_async_copy(src, dst, local_sem.at[i])
        for i, (src, dst) in enumerate([(x_hbm, x_in), (g_hbm, g_in), (high_hbm, high), (low_hbm, low)])
    ]
    for load in loads:
        load.start()

    barrier = pltpu.get_barrier_semaphore()
    for d in range(1, SEQ):
        pl.semaphore_signal(barrier, inc=1, device_id=((s + d) % SEQ, c), device_id_type=MESH)
    for d in range(1, CHAN):
        pl.semaphore_signal(barrier, inc=1, device_id=(s, (c + d) % CHAN), device_id_type=MESH)

    loads[0].wait()
    loads[1].wait()

    def a2a(slot, peer):
        return pltpu.make_async_remote_copy(
            src_ref=send.at[peer], dst_ref=recv.at[slot], send_sem=a2a_send.at[peer], recv_sem=a2a_recv.at[slot],
            device_id=(peer, c), device_id_type=MESH,
        )

    for t in range(SEQ_SIDE):
        plane = (z + (2, 1, 3, 0)[t]) % SEQ_SIDE
        lanes = pl.ds(pl.multiple_of(plane * 128, 128), 128)
        send[pl.ds(plane * SEQ_SIDE, SEQ_SIDE), 0:OWN, :] = x_in[:, lanes].T.reshape(SEQ_SIDE, OWN, BLOCK)
        send[pl.ds(plane * SEQ_SIDE, SEQ_SIDE), OWN : 2 * OWN, :] = g_in[:, lanes].T.reshape(SEQ_SIDE, OWN, BLOCK)
        if t == 0:
            pl.semaphore_wait(barrier, SEQ + CHAN - 2)
        for k in range(SEQ_SIDE if t < 3 else SEQ_SIDE - 1):
            peer = plane * SEQ_SIDE + (y + (2, 1, 3, 0)[k]) % SEQ_SIDE
            a2a(s, peer).start()
    recv[s] = send[s]

    ef_col = column(ef[...])
    mf_col = column(mf[...])
    features = feat[...]
    pre = dot(ew[...], features[:FEATURES, :], 0, 0) + column(eb[...])
    first_pre[...] = pre
    act, slope = sin_cos(ef_col * pre)
    first_act[...] = act
    first_cos[...] = slope
    pre = dot(mw[...], act, 0, 0) + column(mb[...])
    second_pre[...] = pre
    act, slope = sin_cos(mf_col * pre)
    second_act[...] = act
    second_cos[...] = slope
    pick = lax.broadcasted_iota(jnp.int32, (OWN, BLOCK), 1) == lax.broadcasted_iota(jnp.int32, (OWN, BLOCK), 0) + OWN * s
    rates = jnp.sum(jnp.where(pick, dr[...], 0.0), axis=1, keepdims=True)
    picked = jnp.where(pick, 1.0, 0.0).astype(F32)
    head_rows = dot(picked, hw[...], 1, 1)
    head_cols = dot(hw[...], picked, 1, 1)
    shaped[...] = dot(head_rows, act)
    envelope[...] = jnp.exp(-features[0:1, :] * rates)

    loads[2].wait()
    loads[3].wait()
    for t in range(SEQ_SIDE):
        plane = (z + (0, 3, 1, 2)[t]) % SEQ_SIDE
        for k in range(SEQ_SIDE if t > 0 else SEQ_SIDE - 1):
            peer = plane * SEQ_SIDE + (y + (3, 1, 2, 0)[k]) % SEQ_SIDE
            a2a(peer, peer).wait_recv()
        blocks = recv[pl.ds(plane * SEQ_SIDE, SEQ_SIDE)].reshape(SEQ_SIDE * 2 * OWN, BLOCK)

        def transform(j, _):
            lanes = pl.ds(pl.multiple_of(j * 256, 256), 256)
            got = jnp.dot(blocks, high[:, lanes], preferred_element_type=F32)
            got += jnp.dot(blocks, low[:, lanes], preferred_element_type=F32)
            spec[pl.ds(plane * SEQ_SIDE, SEQ_SIDE), :, lanes] = got.reshape(SEQ_SIDE, 2 * OWN, 256)
            return 0

        lax.fori_loop(0, 4, transform, 0)

    def multiply(i, _):
        row = pl.multiple_of(i // 4 * 8, 8)
        lane = pl.multiple_of(i % 4 * 128, 128)
        sign = jnp.where(i % 4 < 2, 1.0, -1.0).astype(F32)
        re, im = pl.ds(lane, 128), pl.ds(lane + BLOCK, 128)
        xs, total_re, total_im = [], [None] * 4, [None] * 4
        for b in range(SEQ):
            xs.append((spec[b, pl.ds(row, 8), re], spec[b, pl.ds(row, 8), im]))
            g_re, g_im = spec[b, pl.ds(row + OWN, 8), re], spec[b, pl.ds(row + OWN, 8), im]
            for m in range(min(b, PARTS) + 1):
                x_re, x_im = xs[b - m]
                add_re = x_re * g_re + x_im * g_im
                add_im = x_re * g_im - x_im * g_re
                total_re[m] = add_re if total_re[m] is None else total_re[m] + add_re
                total_im[m] = add_im if total_im[m] is None else total_im[m] + add_im
        for p in range(PARTS):
            prod[pl.ds(p * OWN + row, 8), re] = total_re[p] + sign * total_im[p + 1]
            prod[pl.ds(p * OWN + row, 8), im] = total_im[p] - sign * total_re[p + 1]
        return 0

    lax.fori_loop(0, 16, multiply, 0)

    weights = prod[...] * (1.0 / BLOCK)
    weights_high = weights.astype(BF16)
    weights_low = (weights - weights_high.astype(F32)).astype(BF16)

    def invert(j, _):
        rows = pl.ds(pl.multiple_of(j * 256, 256), 256)
        got = dot(weights_high, high[rows, :], 1, 1, None)
        got += dot(weights_low, high[rows, :], 1, 1, None)
        got += dot(weights_high, low[rows, :], 1, 1, None)
        for p in range(PARTS):
            lags[:, pl.ds(pl.multiple_of(p * BLOCK + j * 256, 256), 256)] = got[p * OWN : (p + 1) * OWN, :]
        return 0

    lax.fori_loop(0, 2, invert, 0)

    out_delta = lags[...] * envelope[...]
    mine = pl.ds(pl.multiple_of(s * OWN, OWN), OWN)
    head_all[mine, 0:HIDDEN] = dot(out_delta, second_act[...], 1, 1)
    rate_grad = -jnp.sum(out_delta * shaped[...] * feat[0:1, :], axis=1, keepdims=True)
    head_all[mine, HIDDEN:128] = jnp.broadcast_to(rate_grad, (OWN, 128 - HIDDEN))

    def head_copy(slot, peer):
        rows = pl.ds(pl.multiple_of(slot * OWN, OWN), OWN)
        return pltpu.make_async_remote_copy(
            src_ref=head_all.at[rows], dst_ref=head_all.at[rows], send_sem=head_send.at[peer], recv_sem=head_recv.at[slot],
            device_id=(peer, c), device_id_type=MESH,
        )

    for d in range(1, SEQ):
        head_copy(s, (s + d) % SEQ).start()

    second_grad = dot(head_cols, out_delta)
    second_slope = second_grad * second_cos[...]
    second_delta = second_slope * mf_col
    ones = feat[FEATURES : FEATURES + 1, :]
    part[:, 0:HIDDEN] = dot(first_act[...], second_delta, 1, 1)
    first_grad = dot(mw[...], second_delta)
    first_slope = first_grad * first_cos[...]
    first_delta = first_slope * ef_col
    part[0:FEATURE_ROWS, HIDDEN:128] = dot(features, first_delta, 1, 1)
    ones = jnp.broadcast_to(ones, (8, FILTER_LEN))
    part[24:32, HIDDEN:128] = dot(ones, first_slope * first_pre[...], 1, 1)
    part[32:40, HIDDEN:128] = dot(ones, second_delta, 1, 1)
    part[40:48, HIDDEN:128] = dot(ones, second_slope * second_pre[...], 1, 1)
    part[48:64, HIDDEN:128] = jnp.zeros((16, 128 - HIDDEN), F32)

    def sum_copy(slot, peer):
        return pltpu.make_async_remote_copy(
            src_ref=part.at[pl.ds(pl.multiple_of(peer * 8, 8), 8)], dst_ref=sum_recv.at[slot],
            send_sem=sum_send.at[peer], recv_sem=sum_got.at[slot], device_id=(s, peer), device_id_type=MESH,
        )

    for d in range(1, CHAN):
        sum_copy(c, (c + d) % CHAN).start()
    sum_recv[c] = part[pl.ds(pl.multiple_of(c * 8, 8), 8), :]
    for d in range(1, CHAN):
        peer = (c + d) % CHAN
        sum_copy(peer, peer).wait_recv()
    tile[...] = jnp.sum(sum_recv[...], axis=0)

    def tile_copy(slot, peer):
        return pltpu.make_async_remote_copy(
            src_ref=tile, dst_ref=tile_recv.at[slot], send_sem=tile_send.at[peer], recv_sem=tile_got.at[slot],
            device_id=(peer, c), device_id_type=MESH,
        )

    for d in range(1, SEQ):
        tile_copy(s, (s + d) % SEQ).start()
    tile_recv[s] = tile[...]
    for d in range(1, SEQ):
        peer = (s + d) % SEQ
        tile_copy(peer, peer).wait_recv()
    total[c] = jnp.sum(tile_recv[...], axis=0)

    def all_copy(slot, peer):
        return pltpu.make_async_remote_copy(
            src_ref=total.at[slot], dst_ref=total.at[slot], send_sem=all_send.at[peer], recv_sem=all_got.at[slot],
            device_id=(s, peer), device_id_type=MESH,
        )

    for d in range(1, CHAN):
        all_copy(c, (c + d) % CHAN).start()

    for d in range(1, SEQ):
        peer = (s + d) % SEQ
        head_copy(peer, peer).wait_recv()
    turned = head_all[...].T
    hw_out[...] = turned[0:HIDDEN, :]
    dr_out[...] = turned[HIDDEN : HIDDEN + 1, :]

    for d in range(1, CHAN):
        peer = (c + d) % CHAN
        all_copy(peer, peer).wait_recv()
    done = total[...].reshape(HIDDEN, 128)
    mw_out[...] = done[:, 0:HIDDEN]
    ew_out[...] = done[0:FEATURES, HIDDEN:128]
    eb_out[...] = done[FEATURES : FEATURES + 1, HIDDEN:128]
    ef_out[...] = done[24:25, HIDDEN:128]
    mb_out[...] = done[32:33, HIDDEN:128]
    mf_out[...] = done[40:41, HIDDEN:128]

    for d in range(1, SEQ):
        peer = (s + d) % SEQ
        a2a(s, peer).wait_send()
        head_copy(s, peer).wait_send()
        tile_copy(s, peer).wait_send()
    for d in range(1, CHAN):
        peer = (c + d) % CHAN
        sum_copy(c, peer).wait_send()
        all_copy(c, peer).wait_send()


def shards(inputs, out_grad, ew, eb, ef, mw, mb, mf, hw, dr):
    high, low = transform_table()
    row = lambda v: v.reshape(1, -1)
    vmem = pl.BlockSpec(memory_space=pltpu.VMEM)
    anywhere = pl.BlockSpec(memory_space=pl.ANY)
    out = lambda *shape: jax.ShapeDtypeStruct(shape, F32)
    taps = lambda rows: pltpu.VMEM((rows, FILTER_LEN), F32)
    dma = lambda n: pltpu.SemaphoreType.DMA((n,))
    got = pl.pallas_call(
        kernel,
        out_shape=(
            out(FEATURES, HIDDEN), out(1, HIDDEN), out(1, HIDDEN), out(HIDDEN, HIDDEN), out(1, HIDDEN), out(1, HIDDEN),
            out(HIDDEN, BLOCK), out(1, BLOCK),
        ),
        in_specs=[anywhere] * 2 + [vmem] * 8 + [anywhere] * 2 + [vmem],
        out_specs=(vmem,) * 8,
        scratch_shapes=[
            pltpu.VMEM((BLOCK, BLOCK), BF16), pltpu.VMEM((BLOCK, BLOCK), BF16),
            pltpu.VMEM((BLOCK, 2 * BLOCK), BF16), pltpu.VMEM((BLOCK, 2 * BLOCK), BF16),
            pltpu.VMEM((SEQ, 2 * OWN, BLOCK), BF16), pltpu.VMEM((SEQ, 2 * OWN, BLOCK), BF16),
            pltpu.VMEM((SEQ, 2 * OWN, 2 * BLOCK), F32), pltpu.VMEM((PARTS * OWN, 2 * BLOCK), F32),
            taps(OWN),
            taps(HIDDEN), taps(HIDDEN), taps(HIDDEN), taps(HIDDEN), taps(HIDDEN), taps(HIDDEN), taps(OWN), taps(OWN),
            pltpu.VMEM((BLOCK, 128), F32), pltpu.VMEM((HIDDEN, 128), F32), pltpu.VMEM((CHAN, 8, 128), F32),
            pltpu.VMEM((8, 128), F32), pltpu.VMEM((SEQ, 8, 128), F32), pltpu.VMEM((CHAN, 8, 128), F32),
            dma(4), dma(SEQ), dma(SEQ), dma(SEQ), dma(SEQ), dma(CHAN), dma(CHAN), dma(SEQ), dma(SEQ), dma(CHAN), dma(CHAN),
        ],
        compiler_params=pltpu.CompilerParams(
            collective_id=0, has_side_effects=True, vmem_limit_bytes=40 * 1024 * 1024
        ),
    )(
        inputs, out_grad, ew, row(eb), row(ef), mw, row(mb), row(mf), hw, row(dr),
        jnp.asarray(high), jnp.asarray(low), jnp.asarray(tap_table()),
    )
    ew_g, eb_g, ef_g, mw_g, mb_g, mf_g, hw_g, dr_g = got
    flat = lambda v: v.reshape(-1)
    return ew_g, flat(eb_g), flat(ef_g), mw_g, flat(mb_g), flat(mf_g), hw_g, flat(dr_g)


def solution(mesh):
    return jax.shard_map(
        shards,
        mesh=mesh,
        in_specs=(
            P("seq", "chan"), P("seq", "chan"), P(), P(), P(), P(), P(), P(), P(None, "chan"), P("chan"),
        ),
        out_specs=(P(), P(), P(), P(), P(), P(), P(None, "chan"), P("chan")),
        check_vma=False,
    )
```

profile of v0, /device:TPU:1, one launch (start us, length us, event | category | flops | bytes accessed | tf_op | source)
XLA Modules:
  0.0 60.1 jit_solution(683902269723069918)
XLA Ops:
  0.6 0.0 copy-start.12
  0.6 0.0 copy-start.8
  0.7 0.0 copy-start.9
  0.7 0.0 copy-start.10
  0.7 0.0 copy-start.11
  0.7 0.6 %copy-done.12 = f32[64]{0:T(128)S(1)} copy-done((f32[64]{0:T(128)S(1)}, f32[64]{0:T(128)}, u32[]{:S(2)}) %copy-start.12) | copy-done | bytes 280
  1.3 0.0 copy-done.8
  1.3 0.0 copy-done.9
  1.3 0.0 copy-done.10
  1.3 0.0 copy-done.11
  1.4 0.0 copy-start
  1.4 1.2 %copy-done = bf16[512,1024]{1,0:T(8,128)(2,1)S(1)} copy-done((bf16[512,1024]{1,0:T(8,128)(2,1)S(1)}, bf16[512,1024]{1,0:T(8,128)(2,1)}, u32[]{:S(2)}) %copy-start) | copy-done | bytes 1048600
  2.6 0.0 copy-start.1
  2.6 1.2 %copy-done.1 = bf16[512,1024]{1,0:T(8,128)(2,1)S(1)} copy-done((bf16[512,1024]{1,0:T(8,128)(2,1)S(1)}, bf16[512,1024]{1,0:T(8,128)(2,1)}, u32[]{:S(2)}) %copy-start.1) | copy-done | bytes 1048600
  3.8 0.0 copy-start.2
  3.8 1.0 %copy-done.2 = bf16[512,512]{1,0:T(8,128)(2,1)S(1)} copy-done((bf16[512,512]{1,0:T(8,128)(2,1)S(1)}, bf16[512,512]{1,0:T(8,128)(2,1)}, u32[]{:S(2)}) %copy-start.2) | copy-done | bytes 524312
  4.8 0.0 copy-start.3
  4.9 1.0 %copy-done.3 = bf16[512,512]{1,0:T(8,128)(2,1)S(1)} copy-done((bf16[512,512]{1,0:T(8,128)(2,1)S(1)}, bf16[512,512]{1,0:T(8,128)(2,1)}, u32[]{:S(2)}) %copy-start.3) | copy-done | bytes 524312
  5.9 0.0 copy-start.4
  5.9 0.9 %copy-done.4 = f32[24,1536]{1,0:T(8,128)S(1)} copy-done((f32[24,1536]{1,0:T(8,128)S(1)}, f32[24,1536]{1,0:T(8,128)}, u32[]{:S(2)}) %copy-start.4) | copy-done | bytes 147480
  6.8 0.0 copy-start.5
  6.8 0.9 %copy-done.5 = f32[64,512]{1,0:T(8,128)S(1)} copy-done((f32[64,512]{1,0:T(8,128)S(1)}, f32[64,512]{1,0:T(8,128)}, u32[]{:S(2)}) %copy-start.5) | copy-done | bytes 131096
  7.7 0.0 copy-start.6
  7.7 0.8 %copy-done.6 = f32[64,64]{1,0:T(8,128)S(1)} copy-done((f32[64,64]{1,0:T(8,128)S(1)}, f32[64,64]{1,0:T(8,128)}, u32[]{:S(2)}) %copy-start.6) | copy-done | bytes 16408
  8.5 0.0 copy-start.7
  8.5 0.7 %copy-done.7 = f32[17,64]{1,0:T(8,128)S(1)} copy-done((f32[17,64]{1,0:T(8,128)S(1)}, f32[17,64]{1,0:T(8,128)}, u32[]{:S(2)}) %copy-start.7) | copy-done | bytes 4376
  9.2 46.4 %shard_map.188 = (f32[17,64]{1,0:T(8,128)S(1)}, f32[1,64]{1,0:T(1,128)S(1)}, f32[1,64]{1,0:T(1,128)S(1)}, f32[64,64]{1,0:T(8,128)S(1)}, f32[1,64]{1,0:T(1,128)S(...) custom-call(bf16[512,512]{1,0:T(8,128)(2,1)S(1)} %copy-done.2, ...), custom_call_target="tpu_custom_call" | custom-call | tf_op jit(solution)/shard_map/pallas_call | solution.py:308
  55.6 0.6 %copy.29 = f32[17,64]{1,0:T(8,128)} copy(f32[17,64]{1,0:T(8,128)S(1)} %get-tuple-element.32) | data formatting | bytes 8704
  56.2 0.5 copy.30
  56.7 0.5 copy.31
  57.2 0.6 %copy.32 = f32[64,64]{1,0:T(8,128)} copy(f32[64,64]{1,0:T(8,128)S(1)} %get-tuple-element.35) | data formatting | bytes 32768
  57.8 0.5 copy.33
  58.3 0.5 copy.34
  58.8 0.7 %copy.35 = f32[64,512]{1,0:T(8,128)} copy(f32[64,512]{1,0:T(8,128)S(1)} %get-tuple-element.38) | data formatting | bytes 262144
  59.5 0.6 copy.36
Async XLA Ops:
  0.6 0.7 %copy-start.12 = (f32[64]{0:T(128)S(1)}, f32[64]{0:T(128)}, u32[]{:S(2)}) copy-start(f32[64]{0:T(128)} %param.20) | copy-start | bytes 772
  0.6 0.7 %copy-start.8 = (f32[512]{0:T(512)S(1)}, f32[512]{0:T(512)}, u32[]{:S(2)}) copy-start(f32[512]{0:T(512)} %param.22) | copy-start | bytes 6148
  0.7 0.7 %copy-start.9 = (f32[64]{0:T(128)S(1)}, f32[64]{0:T(128)}, u32[]{:S(2)}) copy-start(f32[64]{0:T(128)} %param.16) | copy-start | bytes 772
  0.7 0.7 %copy-start.10 = (f32[64]{0:T(128)S(1)}, f32[64]{0:T(128)}, u32[]{:S(2)}) copy-start(f32[64]{0:T(128)} %param.17) | copy-start | bytes 772
  0.7 0.7 %copy-start.11 = (f32[64]{0:T(128)S(1)}, f32[64]{0:T(128)}, u32[]{:S(2)}) copy-start(f32[64]{0:T(128)} %param.19) | copy-start | bytes 772
  1.4 1.2 %copy-start = (bf16[512,1024]{1,0:T(8,128)(2,1)S(1)}, bf16[512,1024]{1,0:T(8,128)(2,1)}, u32[]{:S(2)}) copy-start(bf16[512,1024]{1,0:T(8,128)(2,1)} %constant.7.clone.low_hbm) | copy-start | bytes 3145732
  2.6 1.2 %copy-start.1 = (bf16[512,1024]{1,0:T(8,128)(2,1)S(1)}, bf16[512,1024]{1,0:T(8,128)(2,1)}, u32[]{:S(2)}) copy-start(bf16[512,1024]{1,0:T(8,128)(2,1)} %constant.6.clone.high_hbm) | copy-start | bytes 3145732
  3.8 1.0 %copy-start.2 = (bf16[512,512]{1,0:T(8,128)(2,1)S(1)}, bf16[512,512]{1,0:T(8,128)(2,1)}, u32[]{:S(2)}) copy-start(bf16[512,512]{1,0:T(8,128)(2,1)} %x_hbm.1) | copy-start | bytes 1572868
  4.8 1.0 %copy-start.3 = (bf16[512,512]{1,0:T(8,128)(2,1)S(1)}, bf16[512,512]{1,0:T(8,128)(2,1)}, u32[]{:S(2)}) copy-start(bf16[512,512]{1,0:T(8,128)(2,1)} %g_hbm.1) | copy-start | bytes 1572868
  5.9 0.9 %copy-start.4 = (f32[24,1536]{1,0:T(8,128)S(1)}, f32[24,1536]{1,0:T(8,128)}, u32[]{:S(2)}) copy-start(f32[24,1536]{1,0:T(8,128)} %constant.8.clone.feat) | copy-start | bytes 442372
  6.8 0.9 %copy-start.5 = (f32[64,512]{1,0:T(8,128)S(1)}, f32[64,512]{1,0:T(8,128)}, u32[]{:S(2)}) copy-start(f32[64,512]{1,0:T(8,128)} %hw.1) | copy-start | bytes 393220
  7.7 0.8 %copy-start.6 = (f32[64,64]{1,0:T(8,128)S(1)}, f32[64,64]{1,0:T(8,128)}, u32[]{:S(2)}) copy-start(f32[64,64]{1,0:T(8,128)} %mw.1) | copy-start | bytes 49156
  8.5 0.7 %copy-start.7 = (f32[17,64]{1,0:T(8,128)S(1)}, f32[17,64]{1,0:T(8,128)}, u32[]{:S(2)}) copy-start(f32[17,64]{1,0:T(8,128)} %ew.1) | copy-start | bytes 13060
where the time goes:
time: 60.5 us; the launch traced here: 60.1 us
  Pallas kernels  46.4 us (77%)
  local copies, waits for them, and re-layouts  13 us (21%)
  between operations  0.7 us (1%)
    pallas_call x1, Pallas kernels, shards(): pl.pallas_call(kernel, out_shape=(out(FEATURES, HIDDEN), out(1, HIDDEN),...  46.4 us
    unnamed x34, local copies, waits for them, and re-layouts  13 us

commit v1 on v0

--- a/solution.py
+++ b/solution.py
@@ -24,6 +24,7 @@
 OWN = 32
 PARTS = 3
 SEQ_SIDE = 4
+VMEM_LIMIT = 60 * 1024 * 1024
 
 
 def transform_table():
@@ -78,9 +79,9 @@
 
 
 def kernel(
-    x_hbm, g_hbm, ew, eb, ef, mw, mb, mf, hw, dr, high_hbm, low_hbm, feat,
+    x_hbm, g_hbm, high_hbm, low_hbm, feat_hbm, ew_hbm, eb_hbm, ef_hbm, mw_hbm, mb_hbm, mf_hbm, hw_hbm, dr_hbm,
     ew_out, eb_out, ef_out, mw_out, mb_out, mf_out, hw_out, dr_out,
-    x_in, g_in, high, low, send, recv, spec, prod, lags,
+    x_in, g_in, high, low, feat, ew, eb, ef, mw, mb, mf, hw, dr, send, recv, spec, prod, lags,
     first_pre, first_cos, first_act, second_pre, second_cos, second_act, shaped, envelope,
     head_all, part, sum_recv, tile, tile_recv, total,
     local_sem, a2a_send, a2a_recv, head_send, head_recv, sum_send, sum_got, tile_send, tile_got, all_send, all_got,
@@ -92,7 +93,10 @@
 
     loads = [
         pltpu.make_async_copy(src, dst, local_sem.at[i])
-        for i, (src, dst) in enumerate([(x_hbm, x_in), (g_hbm, g_in), (high_hbm, high), (low_hbm, low)])
+        for i, (src, dst) in enumerate([
+            (x_hbm, x_in), (g_hbm, g_in), (feat_hbm, feat), (ew_hbm, ew), (eb_hbm, eb), (ef_hbm, ef), (mw_hbm, mw),
+            (mb_hbm, mb), (mf_hbm, mf), (hw_hbm, hw), (dr_hbm, dr), (high_hbm, high), (low_hbm, low),
+        ])
     ]
     for load in loads:
         load.start()
@@ -124,6 +128,8 @@
             a2a(s, peer).start()
     recv[s] = send[s]
 
+    for load in loads[2:11]:
+        load.wait()
     ef_col = column(ef[...])
     mf_col = column(mf[...])
     features = feat[...]
@@ -145,8 +151,8 @@
     shaped[...] = dot(head_rows, act)
     envelope[...] = jnp.exp(-features[0:1, :] * rates)
 
-    loads[2].wait()
-    loads[3].wait()
+    loads[11].wait()
+    loads[12].wait()
     for t in range(SEQ_SIDE):
         plane = (z + (0, 3, 1, 2)[t]) % SEQ_SIDE
         for k in range(SEQ_SIDE if t > 0 else SEQ_SIDE - 1):
@@ -297,40 +303,59 @@
         all_copy(c, peer).wait_send()
 
 
+def hand_over(*refs):
+    copies = [pltpu.make_async_copy(refs[i], refs[8 + i], refs[16].at[i]) for i in range(8)]
+    for copy in copies:
+        copy.start()
+    for copy in copies:
+        copy.wait()
+
+
 def shards(inputs, out_grad, ew, eb, ef, mw, mb, mf, hw, dr):
     high, low = transform_table()
     row = lambda v: v.reshape(1, -1)
     vmem = pl.BlockSpec(memory_space=pltpu.VMEM)
     anywhere = pl.BlockSpec(memory_space=pl.ANY)
     out = lambda *shape: jax.ShapeDtypeStruct(shape, F32)
+    shapes = (
+        out(FEATURES, HIDDEN), out(1, HIDDEN), out(1, HIDDEN), out(HIDDEN, HIDDEN), out(1, HIDDEN), out(1, HIDDEN),
+        out(HIDDEN, BLOCK), out(1, BLOCK),
+    )
     taps = lambda rows: pltpu.VMEM((rows, FILTER_LEN), F32)
     dma = lambda n: pltpu.SemaphoreType.DMA((n,))
     got = pl.pallas_call(
         kernel,
-        out_shape=(
-            out(FEATURES, HIDDEN), out(1, HIDDEN), out(1, HIDDEN), out(HIDDEN, HIDDEN), out(1, HIDDEN), out(1, HIDDEN),
-            out(HIDDEN, BLOCK), out(1, BLOCK),
-        ),
-        in_specs=[anywhere] * 2 + [vmem] * 8 + [anywhere] * 2 + [vmem],
+        out_shape=shapes,
+        in_specs=[anywhere] * 13,
         out_specs=(vmem,) * 8,
         scratch_shapes=[
             pltpu.VMEM((BLOCK, BLOCK), BF16), pltpu.VMEM((BLOCK, BLOCK), BF16),
             pltpu.VMEM((BLOCK, 2 * BLOCK), BF16), pltpu.VMEM((BLOCK, 2 * BLOCK), BF16),
+            taps(FEATURE_ROWS), pltpu.VMEM((FEATURES, HIDDEN), F32), pltpu.VMEM((1, HIDDEN), F32), pltpu.VMEM((1, HIDDEN), F32),
+            pltpu.VMEM((HIDDEN, HIDDEN), F32), pltpu.VMEM((1, HIDDEN), F32), pltpu.VMEM((1, HIDDEN), F32),
+            pltpu.VMEM((HIDDEN, BLOCK), F32), pltpu.VMEM((1, BLOCK), F32),
             pltpu.VMEM((SEQ, 2 * OWN, BLOCK), BF16), pltpu.VMEM((SEQ, 2 * OWN, BLOCK), BF16),
             pltpu.VMEM((SEQ, 2 * OWN, 2 * BLOCK), F32), pltpu.VMEM((PARTS * OWN, 2 * BLOCK), F32),
             taps(OWN),
             taps(HIDDEN), taps(HIDDEN), taps(HIDDEN), taps(HIDDEN), taps(HIDDEN), taps(HIDDEN), taps(OWN), taps(OWN),
             pltpu.VMEM((BLOCK, 128), F32), pltpu.VMEM((HIDDEN, 128), F32), pltpu.VMEM((CHAN, 8, 128), F32),
             pltpu.VMEM((8, 128), F32), pltpu.VMEM((SEQ, 8, 128), F32), pltpu.VMEM((CHAN, 8, 128), F32),
-            dma(4), dma(SEQ), dma(SEQ), dma(SEQ), dma(SEQ), dma(CHAN), dma(CHAN), dma(SEQ), dma(SEQ), dma(CHAN), dma(CHAN),
+            dma(13), dma(SEQ), dma(SEQ), dma(SEQ), dma(SEQ), dma(CHAN), dma(CHAN), dma(SEQ), dma(SEQ), dma(CHAN), dma(CHAN),
         ],
         compiler_params=pltpu.CompilerParams(
-            collective_id=0, has_side_effects=True, vmem_limit_bytes=40 * 1024 * 1024
+            collective_id=0, has_side_effects=True, vmem_limit_bytes=VMEM_LIMIT
         ),
     )(
-        inputs, out_grad, ew, row(eb), row(ef), mw, row(mb), row(mf), hw, row(dr),
-        jnp.asarray(high), jnp.asarray(low), jnp.asarray(tap_table()),
+        inputs, out_grad, jnp.asarray(high), jnp.asarray(low), jnp.asarray(tap_table()),
+        ew, row(eb), row(ef), mw, row(mb), row(mf), hw, row(dr),
     )
+    got = pl.pallas_call(
+        hand_over,
+        out_shape=shapes,
+        in_specs=[anywhere] * 8,
+        out_specs=(anywhere,) * 8,
+        scratch_shapes=[dma(8)],
+    )(*got)
     ew_g, eb_g, ef_g, mw_g, mb_g, mf_g, hw_g, dr_g = got
     flat = lambda v: v.reshape(-1)
     return ew_g, flat(eb_g), flat(ef_g), mw_g, flat(mb_g), flat(mf_g), hw_g, flat(dr_g)

time: 60.5 us -> 54.2 us (0.90)
  local copies, waits for them, and re-layouts: 13 us -> 0 us
  Pallas kernels: 46.4 us -> 53.5 us
    unnamed x34 -> x0, local copies, waits for them, and re-layouts: 13 us -> none
    pallas_call x1 -> x2, Pallas kernels: 46.4 us -> 53.5 us  [the longest x1 47 us: shards(): pl.pallas_call(kernel, out_shape=shapes, in_specs=[anywhere] * 13, out_sp...]
where the time goes in v1:
time: 54.2 us; the launch traced here: 54.1 us
  Pallas kernels  53.5 us (99%)
  between operations  0.64 us (1%)
    pallas_call x1, Pallas kernels, shards(): pl.pallas_call(kernel, out_shape=shapes, in_specs=[anywhere] * 13, out_sp...  47 us
    pallas_call x1, Pallas kernels, shards(): pl.pallas_call(hand_over, out_shape=shapes, in_specs=[anywhere] * 8, out_...  6.53 us

profile of v1, /device:TPU:1, one launch (start us, length us, event | category | flops | bytes accessed | tf_op | source)
XLA Modules:
  0.0 54.1 jit_solution(14120402199717734616)
XLA Ops:
  0.6 47.0 %shard_map.188 = (f32[17,64]{1,0:T(8,128)}, f32[1,64]{1,0:T(1,128)}, f32[1,64]{1,0:T(1,128)}, f32[64,64]{1,0:T(8,128)}, f32[1,64]{1,0:T(1,128)}, /*index=5*/f32[...) custom-call(bf16[512,512]{1,0:T(8,128)(2,1)} %x_hbm.1, bf16[512,512]{1,0:T(8,128)(2,1)} %g_hbm.1, ...), custom_call_target="tpu_custom_call" | custom-call | tf_op jit(solution)/shard_map/pallas_call | solution.py:326
  47.6 6.5 %shard_map.189 = (f32[17,64]{1,0:T(8,128)}, f32[1,64]{1,0:T(1,128)}, f32[1,64]{1,0:T(1,128)}, f32[64,64]{1,0:T(8,128)}, f32[1,64]{1,0:T(1,128)}, /*index=5*/f32[...) custom-call(f32[17,64]{1,0:T(8,128)} %get-tuple-element.24.refs_0_, f32[1,64]{1,0:T(1,128)} %get-tuple-element.25.refs_1_, ...), custom_call_target="tpu_custom_call" | custom-call | tf_op jit(solution)/shard_map/pallas_call | solution.py:352

commit v2 on v1

--- a/solution.py
+++ b/solution.py
@@ -34,7 +34,14 @@
     table = np.concatenate([np.cos(angle), -np.sin(angle)], axis=1)
     high = table.astype(BF16)
     low = (table - high.astype(np.float64)).astype(BF16)
-    return high, low
+    return high, low, np.ascontiguousarray(high.T), np.ascontiguousarray(low.T)
+
+
+OFFSETS = sorted(
+    [(dz, dy) for dz in range(4) for dy in range(4) if dz or dy],
+    key=lambda o: -(min(o[0], 4 - o[0]) + min(o[1], 4 - o[1])),
+)
+GROUPS = (0, 4, 9, 13, 15)
 
 
 def tap_table():
@@ -52,6 +59,21 @@
 def dot(a, b, a_dim=1, b_dim=0, precision=EXACT):
     return lax.dot_general(
         a, b, (((a_dim,), (b_dim,)), ((), ())), precision=precision, preferred_element_type=F32
+    )
+
+
+def halves(v):
+    high = v.astype(BF16)
+    return high, (v - high.astype(F32)).astype(BF16)
+
+
+def dot3(a, b, a_dim=1, b_dim=0):
+    a_high, a_low = a
+    b_high, b_low = b
+    return (
+        dot(a_high, b_high, a_dim, b_dim, None)
+        + dot(a_high, b_low, a_dim, b_dim, None)
+        + dot(a_low, b_high, a_dim, b_dim, None)
     )
 
 
@@ -79,9 +101,9 @@
 
 
 def kernel(
-    x_hbm, g_hbm, high_hbm, low_hbm, feat_hbm, ew_hbm, eb_hbm, ef_hbm, mw_hbm, mb_hbm, mf_hbm, hw_hbm, dr_hbm,
+    x_hbm, g_hbm, high_hbm, low_hbm, inv_high_hbm, inv_low_hbm, feat_hbm, ew_hbm, eb_hbm, ef_hbm, mw_hbm, mb_hbm, mf_hbm, hw_hbm, dr_hbm,
     ew_out, eb_out, ef_out, mw_out, mb_out, mf_out, hw_out, dr_out,
-    x_in, g_in, high, low, feat, ew, eb, ef, mw, mb, mf, hw, dr, send, recv, spec, prod, lags,
+    x_in, g_in, high, low, inv_high, inv_low, feat, ew, eb, ef, mw, mb, mf, hw, dr, send, recv, spec, prod, lags,
     first_pre, first_cos, first_act, second_pre, second_cos, second_act, shaped, envelope,
     head_all, part, sum_recv, tile, tile_recv, total,
     local_sem, a2a_send, a2a_recv, head_send, head_recv, sum_send, sum_got, tile_send, tile_got, all_send, all_got,
@@ -96,6 +118,7 @@
         for i, (src, dst) in enumerate([
             (x_hbm, x_in), (g_hbm, g_in), (feat_hbm, feat), (ew_hbm, ew), (eb_hbm, eb), (ef_hbm, ef), (mw_hbm, mw),
             (mb_hbm, mb), (mf_hbm, mf), (hw_hbm, hw), (dr_hbm, dr), (high_hbm, high), (low_hbm, low),
+            (inv_high_hbm, inv_high), (inv_low_hbm, inv_low),
         ])
     ]
     for load in loads:
@@ -107,26 +130,25 @@
     for d in range(1, CHAN):
         pl.semaphore_signal(barrier, inc=1, device_id=(s, (c + d) % CHAN), device_id_type=MESH)
 
+    def a2a(k, peer):
+        return pltpu.make_async_remote_copy(
+            src_ref=send.at[peer], dst_ref=recv.at[k], send_sem=a2a_send.at[k], recv_sem=a2a_recv.at[k],
+            device_id=(peer, c), device_id_type=MESH,
+        )
+
+    def target(k):
+        return (z + OFFSETS[k][0]) % SEQ_SIDE * SEQ_SIDE + (y + OFFSETS[k][1]) % SEQ_SIDE
+
+    def source(k):
+        return (z - OFFSETS[k][0] + SEQ_SIDE) % SEQ_SIDE * SEQ_SIDE + (y - OFFSETS[k][1] + SEQ_SIDE) % SEQ_SIDE
+
     loads[0].wait()
     loads[1].wait()
-
-    def a2a(slot, peer):
-        return pltpu.make_async_remote_copy(
-            src_ref=send.at[peer], dst_ref=recv.at[slot], send_sem=a2a_send.at[peer], recv_sem=a2a_recv.at[slot],
-            device_id=(peer, c), device_id_type=MESH,
-        )
-
     for t in range(SEQ_SIDE):
-        plane = (z + (2, 1, 3, 0)[t]) % SEQ_SIDE
-        lanes = pl.ds(pl.multiple_of(plane * 128, 128), 128)
-        send[pl.ds(plane * SEQ_SIDE, SEQ_SIDE), 0:OWN, :] = x_in[:, lanes].T.reshape(SEQ_SIDE, OWN, BLOCK)
-        send[pl.ds(plane * SEQ_SIDE, SEQ_SIDE), OWN : 2 * OWN, :] = g_in[:, lanes].T.reshape(SEQ_SIDE, OWN, BLOCK)
-        if t == 0:
-            pl.semaphore_wait(barrier, SEQ + CHAN - 2)
-        for k in range(SEQ_SIDE if t < 3 else SEQ_SIDE - 1):
-            peer = plane * SEQ_SIDE + (y + (2, 1, 3, 0)[k]) % SEQ_SIDE
-            a2a(s, peer).start()
-    recv[s] = send[s]
+        lanes = slice(t * 128, t * 128 + 128)
+        rows = slice(t * SEQ_SIDE, (t + 1) * SEQ_SIDE)
+        send[rows, 0:OWN, :] = x_in[:, lanes].T.reshape(SEQ_SIDE, OWN, BLOCK)
+        send[rows, OWN : 2 * OWN, :] = g_in[:, lanes].T.reshape(SEQ_SIDE, OWN, BLOCK)
 
     for load in loads[2:11]:
         load.wait()
@@ -134,40 +156,53 @@
     mf_col = column(mf[...])
     features = feat[...]
     pre = dot(ew[...], features[:FEATURES, :], 0, 0) + column(eb[...])
+    act, slope = sin_cos(ef_col * pre)
     first_pre[...] = pre
-    act, slope = sin_cos(ef_col * pre)
-    first_act[...] = act
     first_cos[...] = slope
+    first_act[0, 0:HIDDEN, :], first_act[1, 0:HIDDEN, :] = halves(act)
+    first_act[0, HIDDEN:, :] = jnp.ones((16, FILTER_LEN), BF16)
+    first_act[1, HIDDEN:, :] = jnp.zeros((16, FILTER_LEN), BF16)
     pre = dot(mw[...], act, 0, 0) + column(mb[...])
+    act, slope = sin_cos(mf_col * pre)
     second_pre[...] = pre
-    act, slope = sin_cos(mf_col * pre)
-    second_act[...] = act
     second_cos[...] = slope
+    second_act[0], second_act[1] = halves(act)
     pick = lax.broadcasted_iota(jnp.int32, (OWN, BLOCK), 1) == lax.broadcasted_iota(jnp.int32, (OWN, BLOCK), 0) + OWN * s
     rates = jnp.sum(jnp.where(pick, dr[...], 0.0), axis=1, keepdims=True)
     picked = jnp.where(pick, 1.0, 0.0).astype(F32)
     head_rows = dot(picked, hw[...], 1, 1)
-    head_cols = dot(hw[...], picked, 1, 1)
-    shaped[...] = dot(head_rows, act)
+    head_cols = halves(dot(hw[...], picked, 1, 1))
+    shaped[...] = dot(head_rows, act) * features[0:1, :]
     envelope[...] = jnp.exp(-features[0:1, :] * rates)
 
+    pl.semaphore_wait(barrier, SEQ + CHAN - 2)
+    for k in range(SEQ - 1):
+        a2a(k, target(k)).start()
+
+    recv[SEQ - 1] = send[s]
     loads[11].wait()
     loads[12].wait()
-    for t in range(SEQ_SIDE):
-        plane = (z + (0, 3, 1, 2)[t]) % SEQ_SIDE
-        for k in range(SEQ_SIDE if t > 0 else SEQ_SIDE - 1):
-            peer = plane * SEQ_SIDE + (y + (3, 1, 2, 0)[k]) % SEQ_SIDE
-            a2a(peer, peer).wait_recv()
-        blocks = recv[pl.ds(plane * SEQ_SIDE, SEQ_SIDE)].reshape(SEQ_SIDE * 2 * OWN, BLOCK)
+    for group in range(len(GROUPS) - 1):
+        slots = list(range(GROUPS[group], GROUPS[group + 1]))
+        for k in slots:
+            a2a(k, source(k)).wait_recv()
+        blocks = recv[slots[0] : slots[-1] + 1].reshape(len(slots) * 2 * OWN, BLOCK)
+        owners = [source(k) for k in slots]
+        if group == 0:
+            blocks = jnp.concatenate([blocks, recv[SEQ - 1]], axis=0)
+            owners.append(s)
 
         def transform(j, _):
             lanes = pl.ds(pl.multiple_of(j * 256, 256), 256)
             got = jnp.dot(blocks, high[:, lanes], preferred_element_type=F32)
             got += jnp.dot(blocks, low[:, lanes], preferred_element_type=F32)
-            spec[pl.ds(plane * SEQ_SIDE, SEQ_SIDE), :, lanes] = got.reshape(SEQ_SIDE, 2 * OWN, 256)
+            for i, owner in enumerate(owners):
+                spec[owner, :, lanes] = got[i * 2 * OWN : (i + 1) * 2 * OWN, :]
             return 0
 
         lax.fori_loop(0, 4, transform, 0)
+    loads[13].wait()
+    loads[14].wait()
 
     def multiply(i, _):
         row = pl.multiple_of(i // 4 * 8, 8)
@@ -191,15 +226,14 @@
 
     lax.fori_loop(0, 16, multiply, 0)
 
-    weights = prod[...] * (1.0 / BLOCK)
-    weights_high = weights.astype(BF16)
-    weights_low = (weights - weights_high.astype(F32)).astype(BF16)
+    weights_high, weights_low = halves(prod[...] * (1.0 / BLOCK))
+    weights = jnp.concatenate([weights_high, weights_low], axis=0)
 
     def invert(j, _):
-        rows = pl.ds(pl.multiple_of(j * 256, 256), 256)
-        got = dot(weights_high, high[rows, :], 1, 1, None)
-        got += dot(weights_low, high[rows, :], 1, 1, None)
-        got += dot(weights_high, low[rows, :], 1, 1, None)
+        lanes = pl.ds(pl.multiple_of(j * 256, 256), 256)
+        both = jnp.dot(weights, inv_high[:, lanes], preferred_element_type=F32)
+        got = both[: PARTS * OWN] + both[PARTS * OWN :]
+        got += jnp.dot(weights_high, inv_low[:, lanes], preferred_element_type=F32)
         for p in range(PARTS):
             lags[:, pl.ds(pl.multiple_of(p * BLOCK + j * 256, 256), 256)] = got[p * OWN : (p + 1) * OWN, :]
         return 0
@@ -207,9 +241,11 @@
     lax.fori_loop(0, 2, invert, 0)
 
     out_delta = lags[...] * envelope[...]
+    delta_halves = halves(out_delta)
+    second_acts = second_act[0], second_act[1]
     mine = pl.ds(pl.multiple_of(s * OWN, OWN), OWN)
-    head_all[mine, 0:HIDDEN] = dot(out_delta, second_act[...], 1, 1)
-    rate_grad = -jnp.sum(out_delta * shaped[...] * feat[0:1, :], axis=1, keepdims=True)
+    head_all[mine, 0:HIDDEN] = dot3(delta_halves, second_acts, 1, 1)
+    rate_grad = -jnp.sum(out_delta * shaped[...], axis=1, keepdims=True)
     head_all[mine, HIDDEN:128] = jnp.broadcast_to(rate_grad, (OWN, 128 - HIDDEN))
 
     def head_copy(slot, peer):
@@ -222,52 +258,55 @@
     for d in range(1, SEQ):
         head_copy(s, (s + d) % SEQ).start()
 
-    second_grad = dot(head_cols, out_delta)
+    second_grad = dot3(head_cols, delta_halves)
     second_slope = second_grad * second_cos[...]
-    second_delta = second_slope * mf_col
-    ones = feat[FEATURES : FEATURES + 1, :]
-    part[:, 0:HIDDEN] = dot(first_act[...], second_delta, 1, 1)
-    first_grad = dot(mw[...], second_delta)
-    first_slope = first_grad * first_cos[...]
-    first_delta = first_slope * ef_col
-    part[0:FEATURE_ROWS, HIDDEN:128] = dot(features, first_delta, 1, 1)
-    ones = jnp.broadcast_to(ones, (8, FILTER_LEN))
-    part[24:32, HIDDEN:128] = dot(ones, first_slope * first_pre[...], 1, 1)
-    part[32:40, HIDDEN:128] = dot(ones, second_delta, 1, 1)
-    part[40:48, HIDDEN:128] = dot(ones, second_slope * second_pre[...], 1, 1)
+    second_delta = halves(second_slope * mf_col)
+    first_slope = dot3(halves(mw[...]), second_delta) * first_cos[...]
+    first_delta = halves(first_slope * ef_col)
+    mixer_grad = dot3((first_act[0], first_act[1]), second_delta, 1, 1)
+    part[:, 0:HIDDEN] = mixer_grad[0:HIDDEN, :]
+    part[0:FEATURE_ROWS, HIDDEN:128] = dot3(halves(features), first_delta, 1, 1)
+    ones = jnp.ones((8, FILTER_LEN), BF16)
+    first_high, first_low = halves(first_slope * first_pre[...])
+    part[24:32, HIDDEN:128] = dot(ones, first_high, 1, 1, None) + dot(ones, first_low, 1, 1, None)
+    part[32:40, HIDDEN:128] = mixer_grad[HIDDEN : HIDDEN + 8, :]
+    second_high, second_low = halves(second_slope * second_pre[...])
+    part[40:48, HIDDEN:128] = dot(ones, second_high, 1, 1, None) + dot(ones, second_low, 1, 1, None)
     part[48:64, HIDDEN:128] = jnp.zeros((16, 128 - HIDDEN), F32)
+
+    def everything(ref, count, sem):
+        some = ref.at[pl.ds(0, count)]
+        pltpu.make_async_remote_copy(
+            src_ref=some, dst_ref=some, send_sem=sem.at[0], recv_sem=sem.at[0], device_id=(s, c), device_id_type=MESH
+        ).wait_recv()
 
     def sum_copy(slot, peer):
         return pltpu.make_async_remote_copy(
             src_ref=part.at[pl.ds(pl.multiple_of(peer * 8, 8), 8)], dst_ref=sum_recv.at[slot],
-            send_sem=sum_send.at[peer], recv_sem=sum_got.at[slot], device_id=(s, peer), device_id_type=MESH,
+            send_sem=sum_send.at[peer], recv_sem=sum_got.at[0], device_id=(s, peer), device_id_type=MESH,
         )
 
     for d in range(1, CHAN):
         sum_copy(c, (c + d) % CHAN).start()
     sum_recv[c] = part[pl.ds(pl.multiple_of(c * 8, 8), 8), :]
-    for d in range(1, CHAN):
-        peer = (c + d) % CHAN
-        sum_copy(peer, peer).wait_recv()
+    everything(sum_recv, CHAN - 1, sum_got)
     tile[...] = jnp.sum(sum_recv[...], axis=0)
 
     def tile_copy(slot, peer):
         return pltpu.make_async_remote_copy(
-            src_ref=tile, dst_ref=tile_recv.at[slot], send_sem=tile_send.at[peer], recv_sem=tile_got.at[slot],
+            src_ref=tile, dst_ref=tile_recv.at[slot], send_sem=tile_send.at[peer], recv_sem=tile_got.at[0],
             device_id=(peer, c), device_id_type=MESH,
         )
 
     for d in range(1, SEQ):
         tile_copy(s, (s + d) % SEQ).start()
     tile_recv[s] = tile[...]
-    for d in range(1, SEQ):
-        peer = (s + d) % SEQ
-        tile_copy(peer, peer).wait_recv()
+    everything(tile_recv, SEQ - 1, tile_got)
     total[c] = jnp.sum(tile_recv[...], axis=0)
 
     def all_copy(slot, peer):
         return pltpu.make_async_remote_copy(
-            src_ref=total.at[slot], dst_ref=total.at[slot], send_sem=all_send.at[peer], recv_sem=all_got.at[slot],
+            src_ref=total.at[slot], dst_ref=total.at[slot], send_sem=all_send.at[peer], recv_sem=all_got.at[0],
             device_id=(s, peer), device_id_type=MESH,
         )
 
@@ -281,9 +320,7 @@
     hw_out[...] = turned[0:HIDDEN, :]
     dr_out[...] = turned[HIDDEN : HIDDEN + 1, :]
 
-    for d in range(1, CHAN):
-        peer = (c + d) % CHAN
-        all_copy(peer, peer).wait_recv()
+    everything(total, CHAN - 1, all_got)
     done = total[...].reshape(HIDDEN, 128)
     mw_out[...] = done[:, 0:HIDDEN]
     ew_out[...] = done[0:FEATURES, HIDDEN:128]
@@ -294,7 +331,7 @@
 
     for d in range(1, SEQ):
         peer = (s + d) % SEQ
-        a2a(s, peer).wait_send()
+        a2a(d - 1, target(d - 1)).wait_send()
         head_copy(s, peer).wait_send()
         tile_copy(s, peer).wait_send()
     for d in range(1, CHAN):
@@ -304,15 +341,12 @@
 
 
 def hand_over(*refs):
-    copies = [pltpu.make_async_copy(refs[i], refs[8 + i], refs[16].at[i]) for i in range(8)]
-    for copy in copies:
-        copy.start()
-    for copy in copies:
-        copy.wait()
+    for i in range(8):
+        refs[8 + i][...] = refs[i][...]
 
 
 def shards(inputs, out_grad, ew, eb, ef, mw, mb, mf, hw, dr):
-    high, low = transform_table()
+    high, low, inv_high, inv_low = transform_table()
     row = lambda v: v.reshape(1, -1)
     vmem = pl.BlockSpec(memory_space=pltpu.VMEM)
     anywhere = pl.BlockSpec(memory_space=pl.ANY)
@@ -326,35 +360,36 @@
     got = pl.pallas_call(
         kernel,
         out_shape=shapes,
-        in_specs=[anywhere] * 13,
+        in_specs=[anywhere] * 15,
         out_specs=(vmem,) * 8,
         scratch_shapes=[
             pltpu.VMEM((BLOCK, BLOCK), BF16), pltpu.VMEM((BLOCK, BLOCK), BF16),
             pltpu.VMEM((BLOCK, 2 * BLOCK), BF16), pltpu.VMEM((BLOCK, 2 * BLOCK), BF16),
+            pltpu.VMEM((2 * BLOCK, BLOCK), BF16), pltpu.VMEM((2 * BLOCK, BLOCK), BF16),
             taps(FEATURE_ROWS), pltpu.VMEM((FEATURES, HIDDEN), F32), pltpu.VMEM((1, HIDDEN), F32), pltpu.VMEM((1, HIDDEN), F32),
             pltpu.VMEM((HIDDEN, HIDDEN), F32), pltpu.VMEM((1, HIDDEN), F32), pltpu.VMEM((1, HIDDEN), F32),
             pltpu.VMEM((HIDDEN, BLOCK), F32), pltpu.VMEM((1, BLOCK), F32),
             pltpu.VMEM((SEQ, 2 * OWN, BLOCK), BF16), pltpu.VMEM((SEQ, 2 * OWN, BLOCK), BF16),
             pltpu.VMEM((SEQ, 2 * OWN, 2 * BLOCK), F32), pltpu.VMEM((PARTS * OWN, 2 * BLOCK), F32),
             taps(OWN),
-            taps(HIDDEN), taps(HIDDEN), taps(HIDDEN), taps(HIDDEN), taps(HIDDEN), taps(HIDDEN), taps(OWN), taps(OWN),
+            taps(HIDDEN), taps(HIDDEN), pltpu.VMEM((2, HIDDEN + 16, FILTER_LEN), BF16),
+            taps(HIDDEN), taps(HIDDEN), pltpu.VMEM((2, HIDDEN, FILTER_LEN), BF16), taps(OWN), taps(OWN),
             pltpu.VMEM((BLOCK, 128), F32), pltpu.VMEM((HIDDEN, 128), F32), pltpu.VMEM((CHAN, 8, 128), F32),
             pltpu.VMEM((8, 128), F32), pltpu.VMEM((SEQ, 8, 128), F32), pltpu.VMEM((CHAN, 8, 128), F32),
-            dma(13), dma(SEQ), dma(SEQ), dma(SEQ), dma(SEQ), dma(CHAN), dma(CHAN), dma(SEQ), dma(SEQ), dma(CHAN), dma(CHAN),
+            dma(15), dma(SEQ), dma(SEQ), dma(SEQ), dma(SEQ), dma(CHAN), dma(1), dma(SEQ), dma(1), dma(CHAN), dma(1),
         ],
         compiler_params=pltpu.CompilerParams(
             collective_id=0, has_side_effects=True, vmem_limit_bytes=VMEM_LIMIT
         ),
     )(
-        inputs, out_grad, jnp.asarray(high), jnp.asarray(low), jnp.asarray(tap_table()),
+        inputs, out_grad, jnp.asarray(high), jnp.asarray(low), jnp.asarray(inv_high), jnp.asarray(inv_low), jnp.asarray(tap_table()),
         ew, row(eb), row(ef), mw, row(mb), row(mf), hw, row(dr),
     )
     got = pl.pallas_call(
         hand_over,
         out_shape=shapes,
-        in_specs=[anywhere] * 8,
-        out_specs=(anywhere,) * 8,
-        scratch_shapes=[dma(8)],
+        in_specs=[vmem] * 8,
+        out_specs=(vmem,) * 8,
     )(*got)
     ew_g, eb_g, ef_g, mw_g, mb_g, mf_g, hw_g, dr_g = got
     flat = lambda v: v.reshape(-1)

time: 54.2 us -> 44.2 us (0.82)
  Pallas kernels: 53.5 us -> 43.4 us
    pallas_call x2, Pallas kernels: 53.5 us -> 43.4 us  [the longest x1 41.8 us: shards(): pl.pallas_call(kernel, out_shape=shapes, in_specs=[anywhere] * 15, out_sp...]
where the time goes in v2:
time: 44.2 us; the launch traced here: 44.1 us
  Pallas kernels  43.4 us (98%)
  between operations  0.64 us (1%)
    pallas_call x1, Pallas kernels, shards(): pl.pallas_call(kernel, out_shape=shapes, in_specs=[anywhere] * 15, out_sp...  41.8 us
    pallas_call x1, Pallas kernels, shards(): pl.pallas_call(hand_over, out_shape=shapes, in_specs=[vmem] * 8, out_spec...  1.66 us

profile of v2, /device:TPU:1, one launch (start us, length us, event | category | flops | bytes accessed | tf_op | source)
XLA Modules:
  0.0 44.1 jit_solution(3188619380481066752)
XLA Ops:
  0.6 41.8 %shard_map.206 = (f32[17,64]{1,0:T(8,128)}, f32[1,64]{1,0:T(1,128)}, f32[1,64]{1,0:T(1,128)}, f32[64,64]{1,0:T(8,128)}, f32[1,64]{1,0:T(1,128)}, /*index=5*/f32[...) custom-call(bf16[512,512]{1,0:T(8,128)(2,1)} %x_hbm.1, bf16[512,512]{1,0:T(8,128)(2,1)} %g_hbm.1, ...), custom_call_target="tpu_custom_call" | custom-call | tf_op jit(solution)/shard_map/pallas_call | solution.py:360
  42.4 1.7 %shard_map.207 = (f32[17,64]{1,0:T(8,128)}, f32[1,64]{1,0:T(1,128)}, f32[1,64]{1,0:T(1,128)}, f32[64,64]{1,0:T(8,128)}, f32[1,64]{1,0:T(1,128)}, /*index=5*/f32[...) custom-call(f32[17,64]{1,0:T(8,128)} %get-tuple-element.24.refs_0_, f32[1,64]{1,0:T(1,128)} %get-tuple-element.25.refs_1_, ...), custom_call_target="tpu_custom_call" | custom-call | tf_op jit(solution)/shard_map/pallas_call | solution.py:388

commit v3 on v2

--- a/solution.py
+++ b/solution.py
@@ -105,8 +105,8 @@
     ew_out, eb_out, ef_out, mw_out, mb_out, mf_out, hw_out, dr_out,
     x_in, g_in, high, low, inv_high, inv_low, feat, ew, eb, ef, mw, mb, mf, hw, dr, send, recv, spec, prod, lags,
     first_pre, first_cos, first_act, second_pre, second_cos, second_act, shaped, envelope,
-    head_all, part, sum_recv, tile, tile_recv, total,
-    local_sem, a2a_send, a2a_recv, head_send, head_recv, sum_send, sum_got, tile_send, tile_got, all_send, all_got,
+    head_all, packed, chan_recv, chan_total, seq_recv,
+    local_sem, a2a_send, a2a_recv, head_send, head_recv, sum_send, sum_got, all_send, all_got,
 ):
     s = lax.axis_index("seq")
     c = lax.axis_index("chan")
@@ -149,6 +149,10 @@
         rows = slice(t * SEQ_SIDE, (t + 1) * SEQ_SIDE)
         send[rows, 0:OWN, :] = x_in[:, lanes].T.reshape(SEQ_SIDE, OWN, BLOCK)
         send[rows, OWN : 2 * OWN, :] = g_in[:, lanes].T.reshape(SEQ_SIDE, OWN, BLOCK)
+
+    pl.semaphore_wait(barrier, SEQ + CHAN - 2)
+    for k in range(SEQ - 1):
+        a2a(k, target(k)).start()
 
     for load in loads[2:11]:
         load.wait()
@@ -175,10 +179,6 @@
     shaped[...] = dot(head_rows, act) * features[0:1, :]
     envelope[...] = jnp.exp(-features[0:1, :] * rates)
 
-    pl.semaphore_wait(barrier, SEQ + CHAN - 2)
-    for k in range(SEQ - 1):
-        a2a(k, target(k)).start()
-
     recv[SEQ - 1] = send[s]
     loads[11].wait()
     loads[12].wait()
@@ -192,15 +192,12 @@
             blocks = jnp.concatenate([blocks, recv[SEQ - 1]], axis=0)
             owners.append(s)
 
-        def transform(j, _):
-            lanes = pl.ds(pl.multiple_of(j * 256, 256), 256)
+        for j in range(4):
+            lanes = slice(j * 256, j * 256 + 256)
             got = jnp.dot(blocks, high[:, lanes], preferred_element_type=F32)
             got += jnp.dot(blocks, low[:, lanes], preferred_element_type=F32)
             for i, owner in enumerate(owners):
                 spec[owner, :, lanes] = got[i * 2 * OWN : (i + 1) * 2 * OWN, :]
-            return 0
-
-        lax.fori_loop(0, 4, transform, 0)
     loads[13].wait()
     loads[14].wait()
 
@@ -229,16 +226,13 @@
     weights_high, weights_low = halves(prod[...] * (1.0 / BLOCK))
     weights = jnp.concatenate([weights_high, weights_low], axis=0)
 
-    def invert(j, _):
-        lanes = pl.ds(pl.multiple_of(j * 256, 256), 256)
+    for j in range(2):
+        lanes = slice(j * 256, j * 256 + 256)
         both = jnp.dot(weights, inv_high[:, lanes], preferred_element_type=F32)
         got = both[: PARTS * OWN] + both[PARTS * OWN :]
         got += jnp.dot(weights_high, inv_low[:, lanes], preferred_element_type=F32)
         for p in range(PARTS):
-            lags[:, pl.ds(pl.multiple_of(p * BLOCK + j * 256, 256), 256)] = got[p * OWN : (p + 1) * OWN, :]
-        return 0
-
-    lax.fori_loop(0, 2, invert, 0)
+            lags[:, p * BLOCK + j * 256 : p * BLOCK + j * 256 + 256] = got[p * OWN : (p + 1) * OWN, :]
 
     out_delta = lags[...] * envelope[...]
     delta_halves = halves(out_delta)
@@ -264,15 +258,20 @@
     first_slope = dot3(halves(mw[...]), second_delta) * first_cos[...]
     first_delta = halves(first_slope * ef_col)
     mixer_grad = dot3((first_act[0], first_act[1]), second_delta, 1, 1)
-    part[:, 0:HIDDEN] = mixer_grad[0:HIDDEN, :]
-    part[0:FEATURE_ROWS, HIDDEN:128] = dot3(halves(features), first_delta, 1, 1)
+    packed[0:32, 0:HIDDEN] = mixer_grad[0:32, :]
+    packed[0:32, HIDDEN:128] = mixer_grad[32:HIDDEN, :]
+    embed_grad = dot3(halves(features), first_delta, 1, 1)
+    packed[32:48, 0:HIDDEN] = embed_grad[0:16, :]
+    packed[32:40, HIDDEN:128] = embed_grad[16:24, :]
     ones = jnp.ones((8, FILTER_LEN), BF16)
     first_high, first_low = halves(first_slope * first_pre[...])
-    part[24:32, HIDDEN:128] = dot(ones, first_high, 1, 1, None) + dot(ones, first_low, 1, 1, None)
-    part[32:40, HIDDEN:128] = mixer_grad[HIDDEN : HIDDEN + 8, :]
     second_high, second_low = halves(second_slope * second_pre[...])
-    part[40:48, HIDDEN:128] = dot(ones, second_high, 1, 1, None) + dot(ones, second_low, 1, 1, None)
-    part[48:64, HIDDEN:128] = jnp.zeros((16, 128 - HIDDEN), F32)
+    first_freq = dot(ones, first_high, 1, 1, None) + dot(ones, first_low, 1, 1, None)
+    second_freq = dot(ones, second_high, 1, 1, None) + dot(ones, second_low, 1, 1, None)
+    packed[40:41, HIDDEN:128] = first_freq[0:1, :]
+    packed[41:42, HIDDEN:128] = mixer_grad[HIDDEN : HIDDEN + 1, :]
+    packed[42:43, HIDDEN:128] = second_freq[0:1, :]
+    packed[43:48, HIDDEN:128] = jnp.zeros((5, 128 - HIDDEN), F32)
 
     def everything(ref, count, sem):
         some = ref.at[pl.ds(0, count)]
@@ -282,36 +281,25 @@
 
     def sum_copy(slot, peer):
         return pltpu.make_async_remote_copy(
-            src_ref=part.at[pl.ds(pl.multiple_of(peer * 8, 8), 8)], dst_ref=sum_recv.at[slot],
-            send_sem=sum_send.at[peer], recv_sem=sum_got.at[0], device_id=(s, peer), device_id_type=MESH,
+            src_ref=packed, dst_ref=chan_recv.at[slot], send_sem=sum_send.at[peer], recv_sem=sum_got.at[0],
+            device_id=(s, peer), device_id_type=MESH,
         )
 
     for d in range(1, CHAN):
         sum_copy(c, (c + d) % CHAN).start()
-    sum_recv[c] = part[pl.ds(pl.multiple_of(c * 8, 8), 8), :]
-    everything(sum_recv, CHAN - 1, sum_got)
-    tile[...] = jnp.sum(sum_recv[...], axis=0)
-
-    def tile_copy(slot, peer):
+    chan_recv[c] = packed[...]
+    everything(chan_recv, CHAN - 1, sum_got)
+    chan_total[...] = jnp.sum(chan_recv[...], axis=0)
+
+    def all_copy(slot, peer):
         return pltpu.make_async_remote_copy(
-            src_ref=tile, dst_ref=tile_recv.at[slot], send_sem=tile_send.at[peer], recv_sem=tile_got.at[0],
+            src_ref=chan_total, dst_ref=seq_recv.at[slot], send_sem=all_send.at[peer], recv_sem=all_got.at[0],
             device_id=(peer, c), device_id_type=MESH,
         )
 
-    for d in range(1, SEQ):
-        tile_copy(s, (s + d) % SEQ).start()
-    tile_recv[s] = tile[...]
-    everything(tile_recv, SEQ - 1, tile_got)
-    total[c] = jnp.sum(tile_recv[...], axis=0)
-
-    def all_copy(slot, peer):
-        return pltpu.make_async_remote_copy(
-            src_ref=total.at[slot], dst_ref=total.at[slot], send_sem=all_send.at[peer], recv_sem=all_got.at[0],
-            device_id=(s, peer), device_id_type=MESH,
-        )
-
-    for d in range(1, CHAN):
-        all_copy(c, (c + d) % CHAN).start()
+    for k in range(SEQ - 1):
+        all_copy(s, target(k)).start()
+    seq_recv[s] = chan_total[...]
 
     for d in range(1, SEQ):
         peer = (s + d) % SEQ
@@ -320,24 +308,25 @@
     hw_out[...] = turned[0:HIDDEN, :]
     dr_out[...] = turned[HIDDEN : HIDDEN + 1, :]
 
-    everything(total, CHAN - 1, all_got)
-    done = total[...].reshape(HIDDEN, 128)
-    mw_out[...] = done[:, 0:HIDDEN]
-    ew_out[...] = done[0:FEATURES, HIDDEN:128]
-    eb_out[...] = done[FEATURES : FEATURES + 1, HIDDEN:128]
-    ef_out[...] = done[24:25, HIDDEN:128]
-    mb_out[...] = done[32:33, HIDDEN:128]
-    mf_out[...] = done[40:41, HIDDEN:128]
+    everything(seq_recv, SEQ - 1, all_got)
+    done = jnp.sum(seq_recv[...], axis=0)
+    mw_out[0:32, :] = done[0:32, 0:HIDDEN]
+    mw_out[32:HIDDEN, :] = done[0:32, HIDDEN:128]
+    ew_out[0:16, :] = done[32:48, 0:HIDDEN]
+    ew_out[16:17, :] = done[32:33, HIDDEN:128]
+    eb_out[...] = done[33:34, HIDDEN:128]
+    ef_out[...] = done[40:41, HIDDEN:128]
+    mb_out[...] = done[41:42, HIDDEN:128]
+    mf_out[...] = done[42:43, HIDDEN:128]
 
     for d in range(1, SEQ):
         peer = (s + d) % SEQ
         a2a(d - 1, target(d - 1)).wait_send()
         head_copy(s, peer).wait_send()
-        tile_copy(s, peer).wait_send()
+        all_copy(s, peer).wait_send()
     for d in range(1, CHAN):
         peer = (c + d) % CHAN
         sum_copy(c, peer).wait_send()
-        all_copy(c, peer).wait_send()
 
 
 def hand_over(*refs):
@@ -374,9 +363,9 @@
             taps(OWN),
             taps(HIDDEN), taps(HIDDEN), pltpu.VMEM((2, HIDDEN + 16, FILTER_LEN), BF16),
             taps(HIDDEN), taps(HIDDEN), pltpu.VMEM((2, HIDDEN, FILTER_LEN), BF16), taps(OWN), taps(OWN),
-            pltpu.VMEM((BLOCK, 128), F32), pltpu.VMEM((HIDDEN, 128), F32), pltpu.VMEM((CHAN, 8, 128), F32),
-            pltpu.VMEM((8, 128), F32), pltpu.VMEM((SEQ, 8, 128), F32), pltpu.VMEM((CHAN, 8, 128), F32),
-            dma(15), dma(SEQ), dma(SEQ), dma(SEQ), dma(SEQ), dma(CHAN), dma(1), dma(SEQ), dma(1), dma(CHAN), dma(1),
+            pltpu.VMEM((BLOCK, 128), F32), pltpu.VMEM((48, 128), F32), pltpu.VMEM((CHAN, 48, 128), F32),
+            pltpu.VMEM((48, 128), F32), pltpu.VMEM((SEQ, 48, 128), F32),
+            dma(15), dma(SEQ), dma(SEQ), dma(SEQ), dma(SEQ), dma(CHAN), dma(1), dma(SEQ), dma(1),
         ],
         compiler_params=pltpu.CompilerParams(
             collective_id=0, has_side_effects=True, vmem_limit_bytes=VMEM_LIMIT

time: 44.2 us -> 42 us (0.950)
  Pallas kernels: 43.4 us -> 41.2 us
    pallas_call x1, Pallas kernels: 41.8 us -> 39.6 us  [shards(): pl.pallas_call(kernel, out_shape=shapes, in_specs=[anywhere] * 15, out_sp...]
where the time goes in v3:
time: 42 us; the launch traced here: 41.9 us
  Pallas kernels  41.2 us (98%)
  between operations  0.64 us (2%)
    pallas_call x1, Pallas kernels, shards(): pl.pallas_call(kernel, out_shape=shapes, in_specs=[anywhere] * 15, out_sp...  39.6 us
    pallas_call x1, Pallas kernels, shards(): pl.pallas_call(hand_over, out_shape=shapes, in_specs=[vmem] * 8, out_spec...  1.66 us

profile of v3, /device:TPU:1, one launch (start us, length us, event | category | flops | bytes accessed | tf_op | source)
XLA Modules:
  0.0 41.9 jit_solution(10993350593638570202)
XLA Ops:
  0.6 39.6 %shard_map.206 = (f32[17,64]{1,0:T(8,128)}, f32[1,64]{1,0:T(1,128)}, f32[1,64]{1,0:T(1,128)}, f32[64,64]{1,0:T(8,128)}, f32[1,64]{1,0:T(1,128)}, /*index=5*/f32[...) custom-call(bf16[512,512]{1,0:T(8,128)(2,1)} %x_hbm.1, bf16[512,512]{1,0:T(8,128)(2,1)} %g_hbm.1, ...), custom_call_target="tpu_custom_call" | custom-call | tf_op jit(solution)/shard_map/pallas_call | solution.py:349
  40.2 1.7 %shard_map.207 = (f32[17,64]{1,0:T(8,128)}, f32[1,64]{1,0:T(1,128)}, f32[1,64]{1,0:T(1,128)}, f32[64,64]{1,0:T(8,128)}, f32[1,64]{1,0:T(1,128)}, /*index=5*/f32[...) custom-call(f32[17,64]{1,0:T(8,128)} %get-tuple-element.24.refs_0_, f32[1,64]{1,0:T(1,128)} %get-tuple-element.25.refs_1_, ...), custom_call_target="tpu_custom_call" | custom-call | tf_op jit(solution)/shard_map/pallas_call | solution.py:377

commit v4 on v3

--- a/solution.py
+++ b/solution.py
@@ -24,6 +24,7 @@
 OWN = 32
 PARTS = 3
 SEQ_SIDE = 4
+TILES = 4
 VMEM_LIMIT = 60 * 1024 * 1024
 
 
@@ -31,17 +32,19 @@
     order = np.concatenate([np.arange(0, BLOCK, 2), np.arange(1, BLOCK, 2)])
     turns = (2 * order[None, :] + 1) * np.arange(BLOCK)[:, None] % (4 * BLOCK)
     angle = turns * (2.0 * math.pi / (4 * BLOCK))
-    table = np.concatenate([np.cos(angle), -np.sin(angle)], axis=1)
+    table = np.stack([np.cos(angle).reshape(BLOCK, TILES, 128), -np.sin(angle).reshape(BLOCK, TILES, 128)], axis=2)
+    table = table.reshape(BLOCK, 2 * BLOCK)
     high = table.astype(BF16)
     low = (table - high.astype(np.float64)).astype(BF16)
-    return high, low, np.ascontiguousarray(high.T), np.ascontiguousarray(low.T)
+    inverse = lambda t: np.ascontiguousarray((t.astype(np.float32) / BLOCK).astype(BF16).T)
+    return high, low, inverse(high), inverse(low)
 
 
 OFFSETS = sorted(
     [(dz, dy) for dz in range(4) for dy in range(4) if dz or dy],
     key=lambda o: -(min(o[0], 4 - o[0]) + min(o[1], 4 - o[1])),
 )
-GROUPS = (0, 4, 9, 13, 15)
+GROUPS = (0, 5, 10, 13, 15)
 
 
 def tap_table():
@@ -103,11 +106,14 @@
 def kernel(
     x_hbm, g_hbm, high_hbm, low_hbm, inv_high_hbm, inv_low_hbm, feat_hbm, ew_hbm, eb_hbm, ef_hbm, mw_hbm, mb_hbm, mf_hbm, hw_hbm, dr_hbm,
     ew_out, eb_out, ef_out, mw_out, mb_out, mf_out, hw_out, dr_out,
-    x_in, g_in, high, low, inv_high, inv_low, feat, ew, eb, ef, mw, mb, mf, hw, dr, send, recv, spec, prod, lags,
+    x_in, g_in, high, low, inv_high, inv_low, feat, ew, eb, ef, mw, mb, mf, hw, dr, send, recv,
+    spec_0, spec_1, spec_2, spec_3,
     first_pre, first_cos, first_act, second_pre, second_cos, second_act, shaped, envelope,
-    head_all, packed, chan_recv, chan_total, seq_recv,
+    head_all, head_turned, packed, chan_recv, chan_total, seq_recv, done,
     local_sem, a2a_send, a2a_recv, head_send, head_recv, sum_send, sum_got, all_send, all_got,
+    swap_sem, out_sem,
 ):
+    spec = spec_0, spec_1, spec_2, spec_3
     s = lax.axis_index("seq")
     c = lax.axis_index("chan")
     z = s // SEQ_SIDE
@@ -179,6 +185,37 @@
     shaped[...] = dot(head_rows, act) * features[0:1, :]
     envelope[...] = jnp.exp(-features[0:1, :] * rates)
 
+    def transform(tile, blocks, owners):
+        lanes = slice(tile * 256, tile * 256 + 256)
+        got = jnp.dot(blocks, high[:, lanes], preferred_element_type=F32)
+        got += jnp.dot(blocks, low[:, lanes], preferred_element_type=F32)
+        for i, owner in enumerate(owners):
+            spec[tile][owner, :, :] = got[i * 2 * OWN : (i + 1) * 2 * OWN, :]
+
+    def multiply(tile):
+        parts_re, parts_im = [[] for _ in range(PARTS)], [[] for _ in range(PARTS)]
+        for row in range(0, OWN, 8):
+            xs, total_re, total_im = [], [None] * 4, [None] * 4
+            for b in range(SEQ):
+                x_rows, g_rows = slice(row, row + 8), slice(OWN + row, OWN + row + 8)
+                xs.append((spec[tile][b, x_rows, 0:128], spec[tile][b, x_rows, 128:256]))
+                g_re, g_im = spec[tile][b, g_rows, 0:128], spec[tile][b, g_rows, 128:256]
+                for m in range(min(b, PARTS) + 1):
+                    x_re, x_im = xs[b - m]
+                    add_re = x_re * g_re + x_im * g_im
+                    add_im = x_re * g_im - x_im * g_re
+                    total_re[m] = add_re if total_re[m] is None else total_re[m] + add_re
+                    total_im[m] = add_im if total_im[m] is None else total_im[m] + add_im
+            for p in range(PARTS):
+                if tile < TILES // 2:
+                    parts_re[p].append(total_re[p] + total_im[p + 1])
+                    parts_im[p].append(total_im[p] - total_re[p + 1])
+                else:
+                    parts_re[p].append(total_re[p] - total_im[p + 1])
+                    parts_im[p].append(total_im[p] + total_re[p + 1])
+        join = lambda parts: jnp.concatenate([v for part in parts for v in part], axis=0)
+        return jnp.concatenate([join(parts_re), join(parts_im)], axis=1)
+
     recv[SEQ - 1] = send[s]
     loads[11].wait()
     loads[12].wait()
@@ -192,49 +229,25 @@
             blocks = jnp.concatenate([blocks, recv[SEQ - 1]], axis=0)
             owners.append(s)
 
-        for j in range(4):
-            lanes = slice(j * 256, j * 256 + 256)
-            got = jnp.dot(blocks, high[:, lanes], preferred_element_type=F32)
-            got += jnp.dot(blocks, low[:, lanes], preferred_element_type=F32)
-            for i, owner in enumerate(owners):
-                spec[owner, :, lanes] = got[i * 2 * OWN : (i + 1) * 2 * OWN, :]
+        if group < len(GROUPS) - 2:
+            for tile in range(TILES):
+                transform(tile, blocks, owners)
     loads[13].wait()
     loads[14].wait()
 
-    def multiply(i, _):
-        row = pl.multiple_of(i // 4 * 8, 8)
-        lane = pl.multiple_of(i % 4 * 128, 128)
-        sign = jnp.where(i % 4 < 2, 1.0, -1.0).astype(F32)
-        re, im = pl.ds(lane, 128), pl.ds(lane + BLOCK, 128)
-        xs, total_re, total_im = [], [None] * 4, [None] * 4
-        for b in range(SEQ):
-            xs.append((spec[b, pl.ds(row, 8), re], spec[b, pl.ds(row, 8), im]))
-            g_re, g_im = spec[b, pl.ds(row + OWN, 8), re], spec[b, pl.ds(row + OWN, 8), im]
-            for m in range(min(b, PARTS) + 1):
-                x_re, x_im = xs[b - m]
-                add_re = x_re * g_re + x_im * g_im
-                add_im = x_re * g_im - x_im * g_re
-                total_re[m] = add_re if total_re[m] is None else total_re[m] + add_re
-                total_im[m] = add_im if total_im[m] is None else total_im[m] + add_im
-        for p in range(PARTS):
-            prod[pl.ds(p * OWN + row, 8), re] = total_re[p] + sign * total_im[p + 1]
-            prod[pl.ds(p * OWN + row, 8), im] = total_im[p] - sign * total_re[p + 1]
-        return 0
-
-    lax.fori_loop(0, 16, multiply, 0)
-
-    weights_high, weights_low = halves(prod[...] * (1.0 / BLOCK))
-    weights = jnp.concatenate([weights_high, weights_low], axis=0)
-
-    for j in range(2):
-        lanes = slice(j * 256, j * 256 + 256)
-        both = jnp.dot(weights, inv_high[:, lanes], preferred_element_type=F32)
-        got = both[: PARTS * OWN] + both[PARTS * OWN :]
-        got += jnp.dot(weights_high, inv_low[:, lanes], preferred_element_type=F32)
-        for p in range(PARTS):
-            lags[:, p * BLOCK + j * 256 : p * BLOCK + j * 256 + 256] = got[p * OWN : (p + 1) * OWN, :]
-
-    out_delta = lags[...] * envelope[...]
+    total = None
+    for tile in range(TILES):
+        transform(tile, blocks, owners)
+        weights_high, weights_low = halves(multiply(tile))
+        weights = jnp.concatenate([weights_high, weights_low], axis=0)
+        rows = slice(tile * 256, tile * 256 + 256)
+        both = jnp.dot(weights, inv_high[rows, :], preferred_element_type=F32)
+        share = both[: PARTS * OWN] + both[PARTS * OWN :]
+        share += jnp.dot(weights_high, inv_low[rows, :], preferred_element_type=F32)
+        total = share if total is None else total + share
+    lags = jnp.concatenate([total[p * OWN : (p + 1) * OWN, :] for p in range(PARTS)], axis=1)
+
+    out_delta = lags * envelope[...]
     delta_halves = halves(out_delta)
     second_acts = second_act[0], second_act[1]
     mine = pl.ds(pl.multiple_of(s * OWN, OWN), OWN)
@@ -258,80 +271,86 @@
     first_slope = dot3(halves(mw[...]), second_delta) * first_cos[...]
     first_delta = halves(first_slope * ef_col)
     mixer_grad = dot3((first_act[0], first_act[1]), second_delta, 1, 1)
-    packed[0:32, 0:HIDDEN] = mixer_grad[0:32, :]
-    packed[0:32, HIDDEN:128] = mixer_grad[32:HIDDEN, :]
     embed_grad = dot3(halves(features), first_delta, 1, 1)
-    packed[32:48, 0:HIDDEN] = embed_grad[0:16, :]
-    packed[32:40, HIDDEN:128] = embed_grad[16:24, :]
     ones = jnp.ones((8, FILTER_LEN), BF16)
     first_high, first_low = halves(first_slope * first_pre[...])
     second_high, second_low = halves(second_slope * second_pre[...])
     first_freq = dot(ones, first_high, 1, 1, None) + dot(ones, first_low, 1, 1, None)
     second_freq = dot(ones, second_high, 1, 1, None) + dot(ones, second_low, 1, 1, None)
-    packed[40:41, HIDDEN:128] = first_freq[0:1, :]
-    packed[41:42, HIDDEN:128] = mixer_grad[HIDDEN : HIDDEN + 1, :]
-    packed[42:43, HIDDEN:128] = second_freq[0:1, :]
-    packed[43:48, HIDDEN:128] = jnp.zeros((5, 128 - HIDDEN), F32)
+    packed[0, :, 0:HIDDEN] = mixer_grad[0:24, :]
+    packed[0, 0:16, HIDDEN:128] = mixer_grad[24:40, :]
+    packed[0, 16:24, HIDDEN:128] = embed_grad[16:24, :]
+    packed[1, :, 0:HIDDEN] = mixer_grad[40:64, :]
+    packed[1, 0:16, HIDDEN:128] = embed_grad[0:16, :]
+    packed[1, 16:17, HIDDEN:128] = first_freq[0:1, :]
+    packed[1, 17:18, HIDDEN:128] = mixer_grad[HIDDEN : HIDDEN + 1, :]
+    packed[1, 18:19, HIDDEN:128] = second_freq[0:1, :]
+    packed[1, 19:24, HIDDEN:128] = jnp.zeros((5, 128 - HIDDEN), F32)
 
     def everything(ref, count, sem):
         some = ref.at[pl.ds(0, count)]
+        return pltpu.make_async_remote_copy(
+            src_ref=some, dst_ref=some, send_sem=sem.at[0], recv_sem=sem.at[0], device_id=(s, c), device_id_type=MESH
+        )
+
+    core = c % 2
+    for d in range(1, CHAN):
+        peer = (c + d) % CHAN
         pltpu.make_async_remote_copy(
-            src_ref=some, dst_ref=some, send_sem=sem.at[0], recv_sem=sem.at[0], device_id=(s, c), device_id_type=MESH
-        ).wait_recv()
-
-    def sum_copy(slot, peer):
-        return pltpu.make_async_remote_copy(
-            src_ref=packed, dst_ref=chan_recv.at[slot], send_sem=sum_send.at[peer], recv_sem=sum_got.at[0],
+            src_ref=packed.at[peer % 2], dst_ref=chan_recv.at[c], send_sem=sum_send.at[0], recv_sem=sum_got.at[0],
             device_id=(s, peer), device_id_type=MESH,
-        )
-
-    for d in range(1, CHAN):
-        sum_copy(c, (c + d) % CHAN).start()
-    chan_recv[c] = packed[...]
-    everything(chan_recv, CHAN - 1, sum_got)
+        ).start()
+    chan_recv[c] = packed[core]
+    everything(chan_recv, CHAN - 1, sum_got).wait_recv()
     chan_total[...] = jnp.sum(chan_recv[...], axis=0)
-
-    def all_copy(slot, peer):
-        return pltpu.make_async_remote_copy(
-            src_ref=chan_total, dst_ref=seq_recv.at[slot], send_sem=all_send.at[peer], recv_sem=all_got.at[0],
-            device_id=(peer, c), device_id_type=MESH,
-        )
-
     for k in range(SEQ - 1):
-        all_copy(s, target(k)).start()
+        pltpu.make_async_remote_copy(
+            src_ref=chan_total, dst_ref=seq_recv.at[s], send_sem=all_send.at[0], recv_sem=all_got.at[0],
+            device_id=(target(k), c), device_id_type=MESH,
+        ).start()
     seq_recv[s] = chan_total[...]
 
     for d in range(1, SEQ):
         peer = (s + d) % SEQ
         head_copy(peer, peer).wait_recv()
-    turned = head_all[...].T
-    hw_out[...] = turned[0:HIDDEN, :]
-    dr_out[...] = turned[HIDDEN : HIDDEN + 1, :]
-
-    everything(seq_recv, SEQ - 1, all_got)
-    done = jnp.sum(seq_recv[...], axis=0)
-    mw_out[0:32, :] = done[0:32, 0:HIDDEN]
-    mw_out[32:HIDDEN, :] = done[0:32, HIDDEN:128]
-    ew_out[0:16, :] = done[32:48, 0:HIDDEN]
-    ew_out[16:17, :] = done[32:33, HIDDEN:128]
-    eb_out[...] = done[33:34, HIDDEN:128]
-    ef_out[...] = done[40:41, HIDDEN:128]
-    mb_out[...] = done[41:42, HIDDEN:128]
-    mf_out[...] = done[42:43, HIDDEN:128]
-
+    head_turned[...] = head_all[...].T
+    head_out = [
+        pltpu.make_async_copy(head_turned.at[0:HIDDEN], hw_out, out_sem.at[0]),
+        pltpu.make_async_copy(head_turned.at[HIDDEN : HIDDEN + 8], dr_out, out_sem.at[1]),
+    ]
+    for copy in head_out:
+        copy.start()
     for d in range(1, SEQ):
-        peer = (s + d) % SEQ
         a2a(d - 1, target(d - 1)).wait_send()
-        head_copy(s, peer).wait_send()
-        all_copy(s, peer).wait_send()
-    for d in range(1, CHAN):
-        peer = (c + d) % CHAN
-        sum_copy(c, peer).wait_send()
+        head_copy(s, (s + d) % SEQ).wait_send()
+    everything(chan_recv, CHAN - 1, sum_send).wait_send()
+
+    everything(seq_recv, SEQ - 1, all_got).wait_recv()
+    done[core] = jnp.sum(seq_recv[...], axis=0)
+    swap = pltpu.make_async_remote_copy(
+        src_ref=done.at[core], dst_ref=done.at[core], send_sem=swap_sem.at[0], recv_sem=swap_sem.at[1],
+        device_id=(s, c + 1 - 2 * core), device_id_type=MESH,
+    )
+    swap.start()
+    everything(seq_recv, SEQ - 1, all_send).wait_send()
+    for copy in head_out:
+        copy.wait()
+    swap.wait()
+    mw_out[0:24, :] = done[0, :, 0:HIDDEN]
+    mw_out[24:40, :] = done[0, 0:16, HIDDEN:128]
+    mw_out[40:64, :] = done[1, :, 0:HIDDEN]
+    ew_out[0:16, :] = done[1, 0:16, HIDDEN:128]
+    ew_out[16:17, :] = done[0, 16:17, HIDDEN:128]
+    eb_out[...] = done[0, 17:18, HIDDEN:128]
+    ef_out[...] = done[1, 16:17, HIDDEN:128]
+    mb_out[...] = done[1, 17:18, HIDDEN:128]
+    mf_out[...] = done[1, 18:19, HIDDEN:128]
 
 
 def hand_over(*refs):
-    for i in range(8):
+    for i in range(7):
         refs[8 + i][...] = refs[i][...]
+    refs[15][...] = refs[7][0:1, :]
 
 
 def shards(inputs, out_grad, ew, eb, ef, mw, mb, mf, hw, dr):
@@ -348,9 +367,9 @@
     dma = lambda n: pltpu.SemaphoreType.DMA((n,))
     got = pl.pallas_call(
         kernel,
-        out_shape=shapes,
+        out_shape=shapes[:7] + (out(8, BLOCK),),
         in_specs=[anywhere] * 15,
-        out_specs=(vmem,) * 8,
+        out_specs=(vmem,) * 6 + (anywhere,) * 2,
         scratch_shapes=[
             pltpu.VMEM((BLOCK, BLOCK), BF16), pltpu.VMEM((BLOCK, BLOCK), BF16),
             pltpu.VMEM((BLOCK, 2 * BLOCK), BF16), pltpu.VMEM((BLOCK, 2 * BLOCK), BF16),
@@ -359,13 +378,13 @@
             pltpu.VMEM((HIDDEN, HIDDEN), F32), pltpu.VMEM((1, HIDDEN), F32), pltpu.VMEM((1, HIDDEN), F32),
             pltpu.VMEM((HIDDEN, BLOCK), F32), pltpu.VMEM((1, BLOCK), F32),
             pltpu.VMEM((SEQ, 2 * OWN, BLOCK), BF16), pltpu.VMEM((SEQ, 2 * OWN, BLOCK), BF16),
-            pltpu.VMEM((SEQ, 2 * OWN, 2 * BLOCK), F32), pltpu.VMEM((PARTS * OWN, 2 * BLOCK), F32),
-            taps(OWN),
+            *[pltpu.VMEM((SEQ, 2 * OWN, 256), F32)] * TILES,
             taps(HIDDEN), taps(HIDDEN), pltpu.VMEM((2, HIDDEN + 16, FILTER_LEN), BF16),
             taps(HIDDEN), taps(HIDDEN), pltpu.VMEM((2, HIDDEN, FILTER_LEN), BF16), taps(OWN), taps(OWN),
-            pltpu.VMEM((BLOCK, 128), F32), pltpu.VMEM((48, 128), F32), pltpu.VMEM((CHAN, 48, 128), F32),
-            pltpu.VMEM((48, 128), F32), pltpu.VMEM((SEQ, 48, 128), F32),
-            dma(15), dma(SEQ), dma(SEQ), dma(SEQ), dma(SEQ), dma(CHAN), dma(1), dma(SEQ), dma(1),
+            pltpu.VMEM((BLOCK, 128), F32), pltpu.VMEM((128, BLOCK), F32), pltpu.VMEM((2, 24, 128), F32),
+            pltpu.VMEM((CHAN, 24, 128), F32), pltpu.VMEM((24, 128), F32), pltpu.VMEM((SEQ, 24, 128), F32),
+            pltpu.VMEM((2, 24, 128), F32),
+            dma(15), dma(SEQ), dma(SEQ), dma(SEQ), dma(SEQ), dma(1), dma(1), dma(1), dma(1), dma(2), dma(2),
         ],
         compiler_params=pltpu.CompilerParams(
             collective_id=0, has_side_effects=True, vmem_limit_bytes=VMEM_LIMIT

time: 42 us -> 40.9 us (0.974)
  Pallas kernels: 41.2 us -> 40.1 us
    pallas_call x1, Pallas kernels: 39.6 us -> 38.4 us  [shards(): pl.pallas_call(kernel, out_shape=shapes[:7] + (out(8, BLOCK),), in_specs=...]
where the time goes in v4:
time: 40.9 us; the launch traced here: 40.7 us
  Pallas kernels  40.1 us (98%)
  between operations  0.64 us (2%)
    pallas_call x1, Pallas kernels, shards(): pl.pallas_call(kernel, out_shape=shapes[:7] + (out(8, BLOCK),), in_specs=...  38.4 us
    pallas_call x1, Pallas kernels, shards(): pl.pallas_call(hand_over, out_shape=shapes, in_specs=[vmem] * 8, out_spec...  1.66 us

profile of v4, /device:TPU:1, one launch (start us, length us, event | category | flops | bytes accessed | tf_op | source)
XLA Modules:
  0.0 40.7 jit_solution(14604557596984083725)
XLA Ops:
  0.6 38.4 %shard_map.206 = (f32[17,64]{1,0:T(8,128)}, f32[1,64]{1,0:T(1,128)}, f32[1,64]{1,0:T(1,128)}, f32[64,64]{1,0:T(8,128)}, f32[1,64]{1,0:T(1,128)}, /*index=5*/f32[...) custom-call(bf16[512,512]{1,0:T(8,128)(2,1)} %x_hbm.1, bf16[512,512]{1,0:T(8,128)(2,1)} %g_hbm.1, ...), custom_call_target="tpu_custom_call" | custom-call | tf_op jit(solution)/shard_map/pallas_call | solution.py:368
  39.1 1.7 %shard_map.207 = (f32[17,64]{1,0:T(8,128)}, f32[1,64]{1,0:T(1,128)}, f32[1,64]{1,0:T(1,128)}, f32[64,64]{1,0:T(8,128)}, f32[1,64]{1,0:T(1,128)}, /*index=5*/f32[...) custom-call(f32[17,64]{1,0:T(8,128)} %get-tuple-element.24.refs_0_, f32[1,64]{1,0:T(1,128)} %get-tuple-element.25.refs_1_, ...), custom_call_target="tpu_custom_call" | custom-call | tf_op jit(solution)/shard_map/pallas_call | solution.py:396

commit v5 on v4

--- a/solution.py
+++ b/solution.py
@@ -40,11 +40,10 @@
     return high, low, inverse(high), inverse(low)
 
 
-OFFSETS = sorted(
-    [(dz, dy) for dz in range(4) for dy in range(4) if dz or dy],
-    key=lambda o: -(min(o[0], 4 - o[0]) + min(o[1], 4 - o[1])),
-)
-GROUPS = (0, 5, 10, 13, 15)
+STRAIGHT = 6
+OFFSETS = [(2, 0), (0, 2), (0, 1), (0, 3), (1, 0), (3, 0)]
+OFFSETS += [(2, 2), (1, 2), (2, 1), (2, 3), (3, 2), (1, 1), (1, 3), (3, 1), (3, 3)]
+GROUPS = (0, 6, 10, 13, 15)
 
 
 def tap_table():
@@ -105,13 +104,13 @@
 
 def kernel(
     x_hbm, g_hbm, high_hbm, low_hbm, inv_high_hbm, inv_low_hbm, feat_hbm, ew_hbm, eb_hbm, ef_hbm, mw_hbm, mb_hbm, mf_hbm, hw_hbm, dr_hbm,
-    ew_out, eb_out, ef_out, mw_out, mb_out, mf_out, hw_out, dr_out,
+    head_out, done_out,
     x_in, g_in, high, low, inv_high, inv_low, feat, ew, eb, ef, mw, mb, mf, hw, dr, send, recv,
     spec_0, spec_1, spec_2, spec_3,
     first_pre, first_cos, first_act, second_pre, second_cos, second_act, shaped, envelope,
-    head_all, head_turned, packed, chan_recv, chan_total, seq_recv, done,
+    head_all, head_turned, packed, chan_recv, chan_total, seq_recv, half,
     local_sem, a2a_send, a2a_recv, head_send, head_recv, sum_send, sum_got, all_send, all_got,
-    swap_sem, out_sem,
+    swap_sem, out_sem, row_sem,
 ):
     spec = spec_0, spec_1, spec_2, spec_3
     s = lax.axis_index("seq")
@@ -130,9 +129,16 @@
     for load in loads:
         load.start()
 
+    def along_z(d):
+        return (z + d) % SEQ_SIDE * SEQ_SIDE + y
+
+    def along_y(d):
+        return z * SEQ_SIDE + (y + d) % SEQ_SIDE
+
     barrier = pltpu.get_barrier_semaphore()
-    for d in range(1, SEQ):
-        pl.semaphore_signal(barrier, inc=1, device_id=((s + d) % SEQ, c), device_id_type=MESH)
+    for d in range(1, SEQ_SIDE):
+        pl.semaphore_signal(barrier, inc=1, device_id=(along_z(d), c), device_id_type=MESH)
+        pl.semaphore_signal(barrier, inc=1, device_id=(along_y(d), c), device_id_type=MESH)
     for d in range(1, CHAN):
         pl.semaphore_signal(barrier, inc=1, device_id=(s, (c + d) % CHAN), device_id_type=MESH)
 
@@ -156,8 +162,13 @@
         send[rows, 0:OWN, :] = x_in[:, lanes].T.reshape(SEQ_SIDE, OWN, BLOCK)
         send[rows, OWN : 2 * OWN, :] = g_in[:, lanes].T.reshape(SEQ_SIDE, OWN, BLOCK)
 
-    pl.semaphore_wait(barrier, SEQ + CHAN - 2)
-    for k in range(SEQ - 1):
+    pl.semaphore_wait(barrier, 2 * (SEQ_SIDE - 1) + CHAN - 1)
+    for d in range(1, SEQ_SIDE):
+        pl.semaphore_signal(row_sem, inc=1, device_id=(along_z(d), c), device_id_type=MESH)
+    for k in range(STRAIGHT):
+        a2a(k, target(k)).start()
+    pl.semaphore_wait(row_sem, SEQ_SIDE - 1)
+    for k in range(STRAIGHT, SEQ - 1):
         a2a(k, target(k)).start()
 
     for load in loads[2:11]:
@@ -314,28 +325,29 @@
         peer = (s + d) % SEQ
         head_copy(peer, peer).wait_recv()
     head_turned[...] = head_all[...].T
-    head_out = [
-        pltpu.make_async_copy(head_turned.at[0:HIDDEN], hw_out, out_sem.at[0]),
-        pltpu.make_async_copy(head_turned.at[HIDDEN : HIDDEN + 8], dr_out, out_sem.at[1]),
-    ]
-    for copy in head_out:
-        copy.start()
+    head_write = pltpu.make_async_copy(head_turned.at[0 : HIDDEN + 8], head_out, out_sem.at[0])
+    head_write.start()
     for d in range(1, SEQ):
         a2a(d - 1, target(d - 1)).wait_send()
         head_copy(s, (s + d) % SEQ).wait_send()
     everything(chan_recv, CHAN - 1, sum_send).wait_send()
 
     everything(seq_recv, SEQ - 1, all_got).wait_recv()
-    done[core] = jnp.sum(seq_recv[...], axis=0)
+    half[...] = jnp.sum(seq_recv[...], axis=0)
     swap = pltpu.make_async_remote_copy(
-        src_ref=done.at[core], dst_ref=done.at[core], send_sem=swap_sem.at[0], recv_sem=swap_sem.at[1],
+        src_ref=half, dst_ref=done_out.at[core], send_sem=swap_sem.at[0], recv_sem=swap_sem.at[1],
         device_id=(s, c + 1 - 2 * core), device_id_type=MESH,
     )
     swap.start()
+    half_write = pltpu.make_async_copy(half, done_out.at[core], out_sem.at[1])
+    half_write.start()
     everything(seq_recv, SEQ - 1, all_send).wait_send()
-    for copy in head_out:
-        copy.wait()
+    head_write.wait()
+    half_write.wait()
     swap.wait()
+
+
+def hand_over(head, done, ew_out, eb_out, ef_out, mw_out, mb_out, mf_out, hw_out, dr_out):
     mw_out[0:24, :] = done[0, :, 0:HIDDEN]
     mw_out[24:40, :] = done[0, 0:16, HIDDEN:128]
     mw_out[40:64, :] = done[1, :, 0:HIDDEN]
@@ -345,12 +357,8 @@
     ef_out[...] = done[1, 16:17, HIDDEN:128]
     mb_out[...] = done[1, 17:18, HIDDEN:128]
     mf_out[...] = done[1, 18:19, HIDDEN:128]
-
-
-def hand_over(*refs):
-    for i in range(7):
-        refs[8 + i][...] = refs[i][...]
-    refs[15][...] = refs[7][0:1, :]
+    hw_out[...] = head[0:HIDDEN, :]
+    dr_out[...] = head[HIDDEN : HIDDEN + 1, :]
 
 
 def shards(inputs, out_grad, ew, eb, ef, mw, mb, mf, hw, dr):
@@ -367,9 +375,9 @@
     dma = lambda n: pltpu.SemaphoreType.DMA((n,))
     got = pl.pallas_call(
         kernel,
-        out_shape=shapes[:7] + (out(8, BLOCK),),
+        out_shape=(out(HIDDEN + 8, BLOCK), out(2, 24, 128)),
         in_specs=[anywhere] * 15,
-        out_specs=(vmem,) * 6 + (anywhere,) * 2,
+        out_specs=(anywhere,) * 2,
         scratch_shapes=[
             pltpu.VMEM((BLOCK, BLOCK), BF16), pltpu.VMEM((BLOCK, BLOCK), BF16),
             pltpu.VMEM((BLOCK, 2 * BLOCK), BF16), pltpu.VMEM((BLOCK, 2 * BLOCK), BF16),
@@ -383,8 +391,8 @@
             taps(HIDDEN), taps(HIDDEN), pltpu.VMEM((2, HIDDEN, FILTER_LEN), BF16), taps(OWN), taps(OWN),
             pltpu.VMEM((BLOCK, 128), F32), pltpu.VMEM((128, BLOCK), F32), pltpu.VMEM((2, 24, 128), F32),
             pltpu.VMEM((CHAN, 24, 128), F32), pltpu.VMEM((24, 128), F32), pltpu.VMEM((SEQ, 24, 128), F32),
-            pltpu.VMEM((2, 24, 128), F32),
-            dma(15), dma(SEQ), dma(SEQ), dma(SEQ), dma(SEQ), dma(1), dma(1), dma(1), dma(1), dma(2), dma(2),
+            pltpu.VMEM((24, 128), F32),
+            dma(15), dma(SEQ), dma(SEQ), dma(SEQ), dma(SEQ), dma(1), dma(1), dma(1), dma(1), dma(2), dma(2), pltpu.SemaphoreType.REGULAR,
         ],
         compiler_params=pltpu.CompilerParams(
             collective_id=0, has_side_effects=True, vmem_limit_bytes=VMEM_LIMIT
@@ -396,7 +404,7 @@
     got = pl.pallas_call(
         hand_over,
         out_shape=shapes,
-        in_specs=[vmem] * 8,
+        in_specs=[vmem] * 2,
         out_specs=(vmem,) * 8,
     )(*got)
     ew_g, eb_g, ef_g, mw_g, mb_g, mf_g, hw_g, dr_g = got

time: 40.9 us -> 39.9 us (0.976)
  Pallas kernels: 40.1 us -> 39.1 us
    pallas_call x2, Pallas kernels: 40.1 us -> 39.1 us  [the longest x1 37.4 us: shards(): pl.pallas_call(kernel, out_shape=(out(HIDDEN + 8, BLOCK), out(2, 24, 128)...]
where the time goes in v5:
time: 39.9 us; the launch traced here: 39.7 us
  Pallas kernels  39.1 us (98%)
  between operations  0.64 us (2%)
    pallas_call x1, Pallas kernels, shards(): pl.pallas_call(kernel, out_shape=(out(HIDDEN + 8, BLOCK), out(2, 24, 128)...  37.4 us
    pallas_call x1, Pallas kernels, shards(): pl.pallas_call(hand_over, out_shape=shapes, in_specs=[vmem] * 2, out_spec...  1.66 us

profile of v5, /device:TPU:1, one launch (start us, length us, event | category | flops | bytes accessed | tf_op | source)
XLA Modules:
  0.0 39.7 jit_solution(7259172899679027673)
XLA Ops:
  0.6 37.4 %shard_map.206 = (f32[72,512]{1,0:T(8,128)}, f32[2,24,128]{2,1,0:T(8,128)}) custom-call(bf16[512,512]{1,0:T(8,128)(2,1)} %x_hbm.1, bf16[512,512]{1,0:T(8,128)(2,1)} %g_hbm.1, bf16[512,1024]{1,0:T(8,128)(2,1)} %constant.10.clone.high_hbm, bf16[512,1024]{1,0:T(8,128)(2,1)} %constant.11.clone.low_hbm, bf16[1024,512]{1,0:T(8,128)(2,1)} %constant.12.clone.inv_high_hbm, ...), custom_call_target="tpu_custom_call" | custom-call | tf_op jit(solution)/shard_map/pallas_call | solution.py:376
  38.1 1.7 %shard_map.207 = (f32[17,64]{1,0:T(8,128)}, f32[1,64]{1,0:T(1,128)}, f32[1,64]{1,0:T(1,128)}, f32[64,64]{1,0:T(8,128)}, f32[1,64]{1,0:T(1,128)}, /*index=5*/f32[...) custom-call(f32[72,512]{1,0:T(8,128)} %get-tuple-element.18.head, f32[2,24,128]{2,1,0:T(8,128)} %get-tuple-element.19.done), custom_call_target="tpu_custom_call" | custom-call | tf_op jit(solution)/shard_map/pallas_call | solution.py:404

commit v6 on v5

--- a/solution.py
+++ b/solution.py
@@ -198,8 +198,8 @@
 
     def transform(tile, blocks, owners):
         lanes = slice(tile * 256, tile * 256 + 256)
-        got = jnp.dot(blocks, high[:, lanes], preferred_element_type=F32)
-        got += jnp.dot(blocks, low[:, lanes], preferred_element_type=F32)
+        table = jnp.concatenate([high[:, lanes], low[:, lanes]], axis=0)
+        got = jnp.dot(jnp.concatenate([blocks, blocks], axis=1), table, preferred_element_type=F32)
         for i, owner in enumerate(owners):
             spec[tile][owner, :, :] = got[i * 2 * OWN : (i + 1) * 2 * OWN, :]
 
@@ -305,8 +305,8 @@
         )
 
     core = c % 2
-    for d in range(1, CHAN):
-        peer = (c + d) % CHAN
+    for dx, swapped in ((2, 1), (1, 1), (3, 1), (2, 0), (1, 0), (3, 0), (0, 1)):
+        peer = (c // 2 + dx) % (CHAN // 2) * 2 + (core + swapped) % 2
         pltpu.make_async_remote_copy(
             src_ref=packed.at[peer % 2], dst_ref=chan_recv.at[c], send_sem=sum_send.at[0], recv_sem=sum_got.at[0],
             device_id=(s, peer), device_id_type=MESH,
@@ -314,7 +314,7 @@
     chan_recv[c] = packed[core]
     everything(chan_recv, CHAN - 1, sum_got).wait_recv()
     chan_total[...] = jnp.sum(chan_recv[...], axis=0)
-    for k in range(SEQ - 1):
+    for k in [*range(STRAIGHT, SEQ - 1), *range(STRAIGHT)]:
         pltpu.make_async_remote_copy(
             src_ref=chan_total, dst_ref=seq_recv.at[s], send_sem=all_send.at[0], recv_sem=all_got.at[0],
             device_id=(target(k), c), device_id_type=MESH,

time: 39.9 us -> 39.3 us (0.985)
  Pallas kernels: 39.1 us -> 38.5 us
    pallas_call x1, Pallas kernels: 37.4 us -> 36.9 us  [shards(): pl.pallas_call(kernel, out_shape=(out(HIDDEN + 8, BLOCK), out(2, 24, 128)...]
where the time goes in v6:
time: 39.3 us; the launch traced here: 39.2 us
  Pallas kernels  38.5 us (98%)
  between operations  0.64 us (2%)
    pallas_call x1, Pallas kernels, shards(): pl.pallas_call(kernel, out_shape=(out(HIDDEN + 8, BLOCK), out(2, 24, 128)...  36.9 us
    pallas_call x1, Pallas kernels, shards(): pl.pallas_call(hand_over, out_shape=shapes, in_specs=[vmem] * 2, out_spec...  1.66 us

profile of v6, /device:TPU:1, one launch (start us, length us, event | category | flops | bytes accessed | tf_op | source)
XLA Modules:
  0.0 39.2 jit_solution(6350509121185916882)
XLA Ops:
  0.6 36.9 %shard_map.206 = (f32[72,512]{1,0:T(8,128)}, f32[2,24,128]{2,1,0:T(8,128)}) custom-call(bf16[512,512]{1,0:T(8,128)(2,1)} %x_hbm.1, bf16[512,512]{1,0:T(8,128)(2,1)} %g_hbm.1, bf16[512,1024]{1,0:T(8,128)(2,1)} %constant.10.clone.high_hbm, bf16[512,1024]{1,0:T(8,128)(2,1)} %constant.11.clone.low_hbm, bf16[1024,512]{1,0:T(8,128)(2,1)} %constant.12.clone.inv_high_hbm, ...), custom_call_target="tpu_custom_call" | custom-call | tf_op jit(solution)/shard_map/pallas_call | solution.py:376
  37.5 1.7 %shard_map.207 = (f32[17,64]{1,0:T(8,128)}, f32[1,64]{1,0:T(1,128)}, f32[1,64]{1,0:T(1,128)}, f32[64,64]{1,0:T(8,128)}, f32[1,64]{1,0:T(1,128)}, /*index=5*/f32[...) custom-call(f32[72,512]{1,0:T(8,128)} %get-tuple-element.18.head, f32[2,24,128]{2,1,0:T(8,128)} %get-tuple-element.19.done), custom_call_target="tpu_custom_call" | custom-call | tf_op jit(solution)/shard_map/pallas_call | solution.py:404

commit v7 on v6

--- a/solution.py
+++ b/solution.py
@@ -126,9 +126,6 @@
             (inv_high_hbm, inv_high), (inv_low_hbm, inv_low),
         ])
     ]
-    for load in loads:
-        load.start()
-
     def along_z(d):
         return (z + d) % SEQ_SIDE * SEQ_SIDE + y
 
@@ -141,6 +138,9 @@
         pl.semaphore_signal(barrier, inc=1, device_id=(along_y(d), c), device_id_type=MESH)
     for d in range(1, CHAN):
         pl.semaphore_signal(barrier, inc=1, device_id=(s, (c + d) % CHAN), device_id_type=MESH)
+
+    for load in loads:
+        load.start()
 
     def a2a(k, peer):
         return pltpu.make_async_remote_copy(

time: 39.3 us -> 39.2 us (level)
  no operation moved by 1% of the time
where the time goes in v7:
time: 39.2 us; the launch traced here: 39.1 us
  Pallas kernels  38.5 us (98%)
  between operations  0.64 us (2%)
    pallas_call x1, Pallas kernels, shards(): pl.pallas_call(kernel, out_shape=(out(HIDDEN + 8, BLOCK), out(2, 24, 128)...  36.8 us
    pallas_call x1, Pallas kernels, shards(): pl.pallas_call(hand_over, out_shape=shapes, in_specs=[vmem] * 2, out_spec...  1.66 us

profile of v7, /device:TPU:1, one launch (start us, length us, event | category | flops | bytes accessed | tf_op | source)
XLA Modules:
  0.0 39.1 jit_solution(193068492855051932)
XLA Ops:
  0.6 36.8 %shard_map.206 = (f32[72,512]{1,0:T(8,128)}, f32[2,24,128]{2,1,0:T(8,128)}) custom-call(bf16[512,512]{1,0:T(8,128)(2,1)} %x_hbm.1, bf16[512,512]{1,0:T(8,128)(2,1)} %g_hbm.1, bf16[512,1024]{1,0:T(8,128)(2,1)} %constant.10.clone.high_hbm, bf16[512,1024]{1,0:T(8,128)(2,1)} %constant.11.clone.low_hbm, bf16[1024,512]{1,0:T(8,128)(2,1)} %constant.12.clone.inv_high_hbm, ...), custom_call_target="tpu_custom_call" | custom-call | tf_op jit(solution)/shard_map/pallas_call | solution.py:376
  37.4 1.7 %shard_map.207 = (f32[17,64]{1,0:T(8,128)}, f32[1,64]{1,0:T(1,128)}, f32[1,64]{1,0:T(1,128)}, f32[64,64]{1,0:T(8,128)}, f32[1,64]{1,0:T(1,128)}, /*index=5*/f32[...) custom-call(f32[72,512]{1,0:T(8,128)} %get-tuple-element.18.head, f32[2,24,128]{2,1,0:T(8,128)} %get-tuple-element.19.done), custom_call_target="tpu_custom_call" | custom-call | tf_op jit(solution)/shard_map/pallas_call | solution.py:404
